TPU v7x, 32 devices: a whole 2x2x4 slice. The times are simulated.
32 devices in a mesh: dp: 16 (over z, y, core), seq: 2 (over x).
Axes of the slice: x: 2, y: 2, z: 4, core: 2. Of those that a mesh axis runs over, the one named last changes fastest.
Arguments:
- tokens: bfloat16 [16, 1024, 768], P('dp', 'seq'), may hold values from -6 to 6
- cotangent: bfloat16 [16, 1024, 768], P('dp', 'seq'), may hold values from -6 to 6
- time_index: int32 [16], P('dp'), may hold values from 0 to 999
- step_table: float32 [1000, 128], replicated, may hold values from -6 to 6
- first_gain: bfloat16 [768], replicated, may hold values from 0.5 to 1.5
- attn_qkv: bfloat16 [768, 2304], replicated, may hold values from -0.21875 to 0.21875
- attn_out: bfloat16 [768, 768], replicated, may hold values from -2.5 to 2.5
- second_gain: bfloat16 [768], replicated, may hold values from 0.5 to 1.5
- mlp_up: bfloat16 [768, 3072], replicated, may hold values from -0.21875 to 0.21875
- up_bias: bfloat16 [3072], replicated, may hold values from -3 to 3
- mlp_down: bfloat16 [3072, 768], replicated, may hold values from -0.109375 to 0.109375
- down_bias: bfloat16 [768], replicated, may hold values from -3 to 3
- ada_weight: bfloat16 [128, 4608], replicated, may hold values from -0.5 to 0.5
- ada_bias: bfloat16 [4608], replicated, may hold values from -3 to 3
Outputs:
- mixed: bfloat16 [16, 1024, 768], P('dp', 'seq')
- tokens_grad: float32 [16, 1024, 768], P('dp', 'seq')
- cond_grad: float32 [16, 128], P('dp')
- first_gain_grad: float32 [768], replicated
- attn_qkv_grad: float32 [768, 2304], P('dp')
- attn_out_grad: float32 [768, 768], P('dp')
- second_gain_grad: float32 [768], replicated
- mlp_up_grad: float32 [768, 3072], P('dp')
- up_bias_grad: float32 [3072], replicated
- mlp_down_grad: float32 [3072, 768], P('dp')
- down_bias_grad: float32 [768], replicated
- ada_weight_grad: float32 [128, 4608], P(None, 'dp')
- ada_bias_grad: float32 [4608], replicated
All inputs are finite; a program needn't handle non-finite values.
Results may differ from a plain program's by a relative error of at most 0.014.
The roundings to bfloat16 on the way count: a program that leaves them out, or rounds other values in their place, can miss the bound.
Values may be sent and summed in bfloat16 or wider, within the bound.
No kernel may reach another device: no remote copies, remote signals or barrier semaphores. Data moves between devices by JAX's collectives and lax.ppermute only.
A program may use at most 192 MiB of HBM per device.

v0:
```python
import jax
import jax.numpy as jnp
from jax import lax
from jax.sharding import PartitionSpec as P

H = 12
HD = 64


highest = lax.Precision.HIGHEST


def norm_mod(inputs, gain, shift, scale):
    center = inputs - jnp.mean(inputs, axis=-1, keepdims=True)
    spread = jnp.mean(center * center, axis=-1, keepdims=True)
    return center * lax.rsqrt(spread + 1e-05) * gain * (1.0 + scale) + shift


def tables(positions, head_dim):
    half_dim = head_dim // 2
    frequency = jnp.exp(
        -jnp.log(10000.0) * (2.0 * jnp.arange(half_dim, dtype=jnp.float32) / head_dim)
    )
    angles = positions.astype(jnp.float32)[:, None] * frequency[None, :]
    return (jnp.cos(angles)[:, None, :], jnp.sin(angles)[:, None, :])


def rotate(heads_in, cosine, sine_table):
    half_dim = heads_in.shape[-1] // 2
    lower_half = heads_in[..., :half_dim]
    upper_half = heads_in[..., half_dim:]
    return jnp.concatenate(
        [
            lower_half * cosine - upper_half * sine_table,
            upper_half * cosine + lower_half * sine_table,
        ],
        -1,
    )


def gelu_tanh(inputs):
    return jax.nn.gelu(inputs, approximate=True)


def outer_sum(left, right):
    return lax.dot_general(
        left, right, (((0,), (0,)), ((), ())), preferred_element_type=jnp.float32
    )


def back_mult(left, right):
    return lax.dot_general(
        left, right, (((1,), (1,)), ((), ())), preferred_element_type=jnp.float32
    )


def per_device(
    tokens,
    cotangent,
    time_index,
    step_table,
    first_gain,
    attn_qkv,
    attn_out,
    second_gain,
    mlp_up,
    up_bias,
    mlp_down,
    down_bias,
    ada_weight,
    ada_bias,
):
    rows_here, pos_here, model_width = tokens.shape
    head_count = H
    head_dim = HD
    seq_rank = lax.axis_index("seq")
    seq_length = pos_here * lax.axis_size("seq")
    scale_factor = head_dim ** (-0.5)
    flat_rows = rows_here * pos_here
    steps_count = step_table.shape[0]
    picks = (time_index[:, None] == jnp.arange(steps_count, dtype=jnp.int32)[None, :]).astype(
        jnp.float32
    )
    embedded = jnp.dot(picks, step_table, precision=highest)
    cond, silu_back = jax.vjp(jax.nn.silu, embedded)
    ada_float = ada_weight.astype(jnp.float32)
    modulation = jnp.dot(cond, ada_float, precision=highest) + ada_bias.astype(jnp.float32)
    blocks = [
        modulation[:, None, index * model_width : (index + 1) * model_width] for index in range(6)
    ]
    shift1, scale1, gate1, shift2, scale2, gate2 = blocks
    inputs_f = tokens.astype(jnp.float32)
    normed, norm_back = jax.vjp(norm_mod, inputs_f, first_gain.astype(jnp.float32), shift1, scale1)
    normed_low = normed.astype(jnp.bfloat16).reshape(flat_rows, model_width)
    projected = jnp.dot(normed_low, attn_qkv, preferred_element_type=jnp.float32).reshape(
        rows_here, pos_here, 3 * model_width
    )
    positions = seq_rank * pos_here + jnp.arange(pos_here, dtype=jnp.int32)
    cosine, sine_table = tables(positions, head_dim)

    def turned(block):
        return rotate(
            block.reshape(rows_here, pos_here, head_count, head_dim), cosine, sine_table
        ).reshape(rows_here, pos_here, model_width)

    def unturned(block):
        return rotate(
            block.reshape(rows_here, pos_here, head_count, head_dim), cosine, -sine_table
        ).reshape(rows_here, pos_here, model_width)

    query_low = turned(projected[..., :model_width]).astype(jnp.bfloat16)
    keys_low = turned(projected[..., model_width : 2 * model_width]).astype(jnp.bfloat16)
    values_low = projected[..., 2 * model_width :].astype(jnp.bfloat16)
    all_keys, all_values = (
        lax.all_gather(keys_low, "seq", axis=1, tiled=True),
        lax.all_gather(values_low, "seq", axis=1, tiled=True),
    )
    query_heads = query_low.reshape(rows_here, pos_here, head_count, head_dim)

    def scored(key_block):
        key_heads = key_block.reshape(rows_here, seq_length, head_count, head_dim)
        return (
            jnp.einsum(
                "bqhd,bkhd->bhqk", query_heads, key_heads, preferred_element_type=jnp.float32
            )
            * scale_factor
        )

    scores = scored(all_keys)
    top_score = jnp.max(scores, axis=-1, keepdims=True)
    totals = jnp.sum(jnp.exp(scores - top_score), axis=-1, keepdims=True)
    log_total = top_score + jnp.log(totals)
    probs_low = jnp.exp(scores - log_total).astype(jnp.bfloat16)
    value_heads = all_values.reshape(rows_here, seq_length, head_count, head_dim)
    attended = jnp.einsum(
        "bhqk,bkhd->bqhd", probs_low, value_heads, preferred_element_type=jnp.float32
    )
    attended_low = attended.reshape(flat_rows, model_width).astype(jnp.bfloat16)
    branch = jnp.dot(attended_low, attn_out, preferred_element_type=jnp.float32).reshape(
        rows_here, pos_here, model_width
    )
    middle = inputs_f + gate1 * branch
    normed2, norm2_back = jax.vjp(norm_mod, middle, second_gain.astype(jnp.float32), shift2, scale2)
    normed2_low = normed2.astype(jnp.bfloat16).reshape(flat_rows, model_width)
    pre_act = jnp.dot(normed2_low, mlp_up, preferred_element_type=jnp.float32) + up_bias.astype(
        jnp.float32
    )
    activated, gelu_back = jax.vjp(gelu_tanh, pre_act)
    activated_low = activated.astype(jnp.bfloat16)
    ffn_out = (
        jnp.dot(activated_low, mlp_down, preferred_element_type=jnp.float32)
        + down_bias.astype(jnp.float32)
    ).reshape(rows_here, pos_here, model_width)
    mixed = (middle + gate2 * ffn_out).astype(jnp.bfloat16)
    grad_out = cotangent.astype(jnp.float32)
    d_gate2 = jnp.sum(grad_out * ffn_out, axis=1)
    d_ffn = (gate2 * grad_out).astype(jnp.bfloat16).reshape(flat_rows, model_width)
    down_bias_grad = jnp.sum(d_ffn, axis=0, dtype=jnp.float32)
    mlp_down_grad = outer_sum(activated_low, d_ffn)
    d_activated = back_mult(d_ffn, mlp_down)
    (d_pre_f,) = gelu_back(d_activated)
    d_pre = d_pre_f.astype(jnp.bfloat16)
    up_bias_grad = jnp.sum(d_pre, axis=0, dtype=jnp.float32)
    mlp_up_grad = outer_sum(normed2_low, d_pre)
    d_normed2 = back_mult(d_pre, mlp_up).reshape(rows_here, pos_here, model_width)
    d_middle_norm, second_gain_grad, d_shift2, d_scale2 = norm2_back(d_normed2)
    d_middle = grad_out + d_middle_norm
    d_gate1 = jnp.sum(d_middle * branch, axis=1)
    d_branch = (gate1 * d_middle).astype(jnp.bfloat16).reshape(flat_rows, model_width)
    attn_out_grad = outer_sum(attended_low, d_branch)
    d_attended = (
        back_mult(d_branch, attn_out)
        .astype(jnp.bfloat16)
        .reshape(rows_here, pos_here, head_count, head_dim)
    )
    back_keys, back_values = (all_keys, all_values)
    scores_again = scored(back_keys)
    probs = jnp.exp(scores_again - log_total)
    probs_again = probs.astype(jnp.bfloat16)
    back_value_heads = back_values.reshape(rows_here, seq_length, head_count, head_dim)
    back_key_heads = back_keys.reshape(rows_here, seq_length, head_count, head_dim)
    d_probs = jnp.einsum(
        "bqhd,bkhd->bhqk", d_attended, back_value_heads, preferred_element_type=jnp.float32
    )
    delta_sum = jnp.sum(probs * d_probs, axis=-1, keepdims=True)
    d_scores = (probs * (d_probs - delta_sum)).astype(jnp.bfloat16)
    d_values_all = jnp.einsum(
        "bhqk,bqhd->bkhd", probs_again, d_attended, preferred_element_type=jnp.float32
    )
    d_query = (
        jnp.einsum("bhqk,bkhd->bqhd", d_scores, back_key_heads, preferred_element_type=jnp.float32)
        * scale_factor
    )
    d_keys_all = (
        jnp.einsum("bhqk,bqhd->bkhd", d_scores, query_heads, preferred_element_type=jnp.float32)
        * scale_factor
    )
    d_keys_own, d_values_own = (
        lax.psum_scatter(
            d_keys_all.reshape(rows_here, seq_length, model_width).astype(jnp.bfloat16),
            "seq",
            scatter_dimension=1,
            tiled=True,
        ).astype(jnp.float32),
        lax.psum_scatter(
            d_values_all.reshape(rows_here, seq_length, model_width).astype(jnp.bfloat16),
            "seq",
            scatter_dimension=1,
            tiled=True,
        ).astype(jnp.float32),
    )
    d_projected = (
        jnp.concatenate(
            [
                unturned(d_query.reshape(rows_here, pos_here, model_width)),
                unturned(d_keys_own),
                d_values_own,
            ],
            -1,
        )
        .astype(jnp.bfloat16)
        .reshape(flat_rows, 3 * model_width)
    )
    attn_qkv_grad = outer_sum(normed_low, d_projected)
    d_normed = back_mult(d_projected, attn_qkv).reshape(rows_here, pos_here, model_width)
    d_inputs, first_gain_grad, d_shift1, d_scale1 = norm_back(d_normed)
    tokens_grad = d_middle + d_inputs
    d_modulation = jnp.concatenate(
        [d_shift1[:, 0], d_scale1[:, 0], d_gate1, d_shift2[:, 0], d_scale2[:, 0], d_gate2], -1
    )
    ada_turned = jnp.dot(d_modulation.T, cond, precision=highest)
    ada_bias_grad = jnp.sum(d_modulation, axis=0)
    d_mod_total = lax.psum(d_modulation, "seq")
    (cond_grad,) = silu_back(jnp.dot(d_mod_total, ada_float.T, precision=highest))
    small_total = lax.psum(
        (first_gain_grad, second_gain_grad, up_bias_grad, down_bias_grad, ada_bias_grad),
        ("dp", "seq"),
    )
    matrices = (attn_qkv_grad, attn_out_grad, mlp_up_grad, mlp_down_grad, ada_turned)
    row_parts = (
        lax.psum_scatter(matrices[0], "dp", scatter_dimension=0, tiled=True),
        lax.psum_scatter(matrices[1], "dp", scatter_dimension=0, tiled=True),
        lax.psum_scatter(matrices[2], "dp", scatter_dimension=0, tiled=True),
        lax.psum_scatter(matrices[3], "dp", scatter_dimension=0, tiled=True),
        lax.psum_scatter(matrices[4], "dp", scatter_dimension=0, tiled=True),
    )
    row_total = (
        lax.psum(row_parts[0].astype(jnp.bfloat16), "seq").astype(jnp.float32),
        lax.psum(row_parts[1].astype(jnp.bfloat16), "seq").astype(jnp.float32),
        lax.psum(row_parts[2].astype(jnp.bfloat16), "seq").astype(jnp.float32),
        lax.psum(row_parts[3].astype(jnp.bfloat16), "seq").astype(jnp.float32),
        lax.psum(row_parts[4].astype(jnp.bfloat16), "seq").astype(jnp.float32),
    )
    return (
        mixed,
        tokens_grad,
        cond_grad,
        small_total[0],
        row_total[0],
        row_total[1],
        small_total[1],
        row_total[2],
        small_total[2],
        row_total[3],
        small_total[3],
        row_total[4].T,
        small_total[4],
    )


def solution(mesh):
    placed = (
        P("dp", "seq", None),
        P("dp", "seq", None),
        P("dp"),
        P(),
        P(),
        P(),
        P(),
        P(),
        P(),
        P(),
        P(),
        P(),
        P(),
        P(),
    )
    return jax.shard_map(
        per_device,
        mesh=mesh,
        in_specs=placed,
        out_specs=(
            P("dp", "seq", None),
            P("dp", "seq", None),
            P("dp", None),
            P(),
            P("dp", None),
            P("dp", None),
            P(),
            P("dp", None),
            P(),
            P("dp", None),
            P(),
            P(None, "dp"),
            P(),
        ),
        check_vma=False,
    )
```

profile of v0, /device:TPU:0, one launch (start us, length us, event | category | flops | bytes accessed | tf_op | source)
XLA Modules:
  0.0 755.1 jit_solution(18331578566707334383)
XLA Ops:
  8.8 1.4 convert_reduce_fusion.1
  10.3 1.5 fusion.27
  11.8 1.9 fusion.72
  15.0 2.2 convolution_bitcast_fusion
  17.2 2.0 fusion.84
  19.2 1.0 copy-done.14
  20.3 3.0 copy.36
  23.3 3.0 copy.37
  26.3 1.6 fusion.57
  27.9 3.2 fusion.52
  32.2 2.4 slice.121
  35.3 1.3 convert_element_type.190
  36.5 25.7 %all-gather.5.cloned.1.call-done = bf16[1,1024,768]{1,2,0:T(8,128)(2,1)} async-done(((bf16[1,512,768]{1,2,0:T(8,128)(2,1)}), bf16[1,1024,768]{1,2,0:T(8,128)(2,1)}) %all-gather.5.cloned.1.call-update) | async-done | bytes 1572880 | tf_op jit(solution)/shard_map/all_gather | solution.py:115
  62.2 14.2 %multiply_reduce_fusion.1 = (f32[12,512]{1,0:T(8,128)S(1)}, f32[12,512,1024]{2,1,0:T(8,128)}) fusion(bf16[1024,12,64]{0,2,1:T(8,128)(2,1)} %bitcast.150, bf16[512,12,32]{0,2,1:T(8,128)(2,1)} %get-tuple-element.49, bf16[512,12,32]{0,2,1:T(8,128)(2,1)} %get-tuple-element.48), kind=kOutput, calls=%fused_computation.4 | convolution fusion | flops 819456000 | bytes 27549696 | tf_op jit(solution)/shard_map/bqhd,bkhd->bhqk/dot_general | solution.py:123
  76.5 11.4 %exponential_reduce_fusion = f32[12,512]{1,0:T(8,128)S(1)} fusion(f32[12,512,1024]{2,1,0:T(8,128)} %get-tuple-element.61, f32[12,512]{1,0:T(8,128)S(1)} %get-tuple-element.60), kind=kLoop, calls=%fused_computation.3 | loop fusion | flops 18868224 | bytes 25214976 | tf_op jit(solution)/shard_map/reduce_sum | solution.py:131
  88.5 3.1 all-gather.3.cloned.1.call-done
  91.6 2.6 copy.35
  94.2 11.2 %fusion.36 = bf16[12,64,512]{2,1,0:T(8,128)(2,1)S(1)} fusion(bf16[1024,12,64]{0,2,1:T(8,128)(2,1)} %bitcast.140, f32[12,512,1024]{2,1,0:T(8,128)} %get-tuple-element.61, f32[12,512]{1,0:T(8,128)} %log_add_fusion), kind=kOutput, calls=%fused_computation.64 | convolution fusion | flops 824573952 | bytes 27549696 | tf_op jit(solution)/shard_map/bhqk,bkhd->bqhd/dot_general | solution.py:135
  105.4 2.0 fusion.83
  108.1 5.6 fusion.79
  113.8 7.2 convert_reduce_fusion
  121.0 3.7 fusion.31
  125.8 1.2 copy-done.9
  127.0 1.8 convolution_convert_fusion
  128.7 2.3 copy.38
  131.1 17.6 %multiply_reduce_fusion = (f32[12,512]{1,0:T(8,128)}, f32[12,512,1024]{2,1,0:T(8,128)}) fusion(f32[12,512,1024]{2,1,0:T(8,128)} %get-tuple-element.61, f32[12,512]{1,0:T(8,128)} %log_add_fusion, bf16[512,12,64]{0,2,1:T(8,128)(2,1)} %bitcast.145, bf16[1024,12,64]{0,2,1:T(8,128)(2,1)} %bitcast.141), kind=kOutput, calls=%fused_computation.1 | convolution fusion | flops 830466048 | bytes 52740096 | tf_op jit(solution)/shard_map/bqhd,bkhd->bhqk/dot_general | solution.py:182
  148.7 17.0 %multiply_convert_fusion = bf16[12,512,1024]{2,1,0:T(8,128)(2,1)S(1)} fusion(f32[12,512,1024]{2,1,0:T(8,128)} %get-tuple-element.65, f32[12,512,1024]{2,1,0:T(8,128)} %get-tuple-element.61, f32[12,512]{1,0:T(8,128)} %get-tuple-element.64, f32[12,512]{1,0:T(8,128)} %log_add_fusion), kind=kLoop, calls=%fused_computation | loop fusion | flops 31457280 | bytes 62963712 | tf_op jit(solution)/shard_map/convert_element_type | solution.py:186
  165.7 4.1 multiply_convert_fusion.2
  170.8 12.7 %fusion.18 = bf16[12,64,1024]{2,1,0:T(8,128)(2,1)} fusion(bf16[512,12,64]{0,2,1:T(8,128)(2,1)} %bitcast.146, f32[12,512,1024]{2,1,0:T(8,128)} %get-tuple-element.61, f32[12,512]{1,0:T(8,128)} %log_add_fusion), kind=kOutput, calls=%fused_computation.36 | convolution fusion | flops 824967168 | bytes 27549696 | tf_op jit(solution)/shard_map/bhqk,bqhd->bkhd/dot_general | solution.py:187
  183.7 1.3 convert_element_type.192
  185.0 2.1 reduce_sum.236
  187.2 4.2 fusion.54
  191.4 10.2 %multiply_bitcast_fusion = f32[1,512,12,64]{1,3,2,0:T(8,128)} fusion(bf16[1024,12,64]{0,2,1:T(8,128)(2,1)} %bitcast.151, bf16[12,512,1024]{2,1,0:T(8,128)(2,1)} %copy-done.1), kind=kOutput, calls=%fused_computation.60 | convolution fusion | flops 805699584 | bytes 15728640 | tf_op jit(solution)/shard_map/bhqk,bkhd->bqhd/dot_general | solution.py:191
  201.7 1.5 convert.46
  203.9 1.4 pad_maximum_fusion.5
  205.3 20.6 %reduce-scatter.10.cloned.1.call-done = bf16[1,512,768]{1,2,0:T(8,128)(2,1)} async-done(((bf16[1,1024,768]{1,2,0:T(8,128)(2,1)}), bf16[1,512,768]{1,2,0:T(8,128)(2,1)}) %reduce-scatter.10.cloned.1.call-update) | async-done | bytes 786448 | tf_op jit(solution)/shard_map/reduce_scatter | solution.py:205
  225.9 5.2 fusion.28
  231.6 2.1 reduce_sum.230
  233.8 3.5 fusion.26
  238.6 11.5 %fusion.30 = (f32[768]{0:T(1024)S(1)}, f32[768]{0:T(1024)S(1)}, f32[1,512,768]{2,1,0:T(8,128)}, bf16[1,512,768]{2,1,0:T(8,128)(2,1)}) fusion(bf16[1,512,768]{2,1,0:T(8,128)(2,1)} %param.15, f32[768]{0:T(1024)S(1)} %copy-done.49, f32[512,768]{1,0:T(8,128)} %get-tuple-element.62, f32[1,512,768]{2,1,0:T(8,128)} %copy-done.9, f32[512]{0:T(512)S(1)} %copy-done.44, ...), kind=kOutput, calls=%fused_computation.46 | convolution fusion | flops 2439903744 | bytes 21274624 | tf_op jit(solution)/shard_map/dot_general | solution.py:151
  252.5 1.4 reduce.31
  253.9 3.5 broadcast_multiply_fusion
  257.7 7.1 fusion.39
  265.5 8.8 %fusion.77 = f32[768,3072]{1,0:T(8,128)} fusion(bf16[512,3072]{1,0:T(8,128)(2,1)} %copy-done.55, f32[1,512,768]{2,1,0:T(8,128)} %copy-done.2, f32[768]{0:T(1024)} %get-tuple-element.22, f32[768]{0:T(1024)S(1)} %copy-done.33, f32[768]{0:T(1024)S(1)} %copy-done.28, f32[512]{0:T(512)S(1)} %copy-done.42, f32[512]{0:T(512)S(1)} %broadcast_multiply_fusion.1), kind=kOutput, calls=%fused_computation.141 | convolution fusion | flops 2418278400 | bytes 14169088 | tf_op jit(solution)/shard_map/dot_general | solution.py:46
  275.0 10.6 %fusion.45 = f32[3072,768]{1,0:T(8,128)} fusion(bf16[1,512,768]{2,1,0:T(8,128)(2,1)} %param.15, f32[768]{0:T(1024)S(1)} %copy-done.31, f32[512,3072]{1,0:T(8,128)} %copy-done.54, f32[3072]{0:T(1024)S(1)} %copy-done.39), kind=kOutput, calls=%fused_computation.88 | convolution fusion | flops 2432827392 | bytes 16530432 | tf_op jit(solution)/shard_map/dot_general | solution.py:46
  285.7 6.8 reduce-scatter.14.cloned.1.call-done
  292.5 1.6 convert_element_type.210
  294.0 64.6 %reduce-scatter.20.cloned.1.call-done = f32[288,128]{1,0:T(8,128)} async-done(((f32[4608,128]{1,0:T(8,128)}), f32[288,128]{1,0:T(8,128)}) %reduce-scatter.20.cloned.1.call-update) | async-done | bytes 147472 | tf_op jit(solution)/shard_map/reduce_scatter | solution.py:245
  358.6 1.6 convert_bitcast_fusion
  360.1 91.6 %reduce-scatter.12.cloned.1.call-done = f32[48,2304]{1,0:T(8,128)} async-done(((f32[768,2304]{1,0:T(8,128)}), f32[48,2304]{1,0:T(8,128)}) %reduce-scatter.12.cloned.1.call-update) | async-done | bytes 442384 | tf_op jit(solution)/shard_map/reduce_scatter | solution.py:241
  451.7 1.7 convert_element_type.208
  453.4 113.8 %reduce-scatter.16.cloned.1.call-done = f32[48,3072]{1,0:T(8,128)} async-done(((f32[768,3072]{1,0:T(8,128)}), f32[48,3072]{1,0:T(8,128)}) %reduce-scatter.16.cloned.1.call-update) | async-done | bytes 589840 | tf_op jit(solution)/shard_map/reduce_scatter | solution.py:243
  567.3 1.8 convert_element_type.212
  569.1 113.4 %reduce-scatter.18.cloned.1.call-done = f32[192,768]{1,0:T(8,128)} async-done(((f32[3072,768]{1,0:T(8,128)}), f32[192,768]{1,0:T(8,128)}) %reduce-scatter.18.cloned.1.call-update) | async-done | bytes 589840 | tf_op jit(solution)/shard_map/reduce_scatter | solution.py:244
  682.5 1.8 convert_element_type.215
  684.4 1.3 convert_reduce_fusion.2
  685.7 9.5 %psum.77 = f32[4608]{0:T(1024)} all-reduce(f32[4608]{0:T(1024)} %reduce.31), channel_id=1, replica_groups=mesh['dp'=16,'seq'=2] {'seq'}, use_global_device_ids=true, to_apply=%region_19.20 | all-reduce | flops 4608 | bytes 36864 | tf_op jit(solution)/shard_map/psum | solution.py:233
  695.1 1.3 reshape.551
  696.5 40.9 %all-reduce = (f32[768]{0:T(1024)}, f32[768]{0:T(1024)}, f32[3072]{0:T(1024)}, f32[768]{0:T(1024)}, f32[4608]{0:T(1024)}) all-reduce(f32[768]{0:T(1024)S(1)} %copy-done.36, f32[768]{0:T(1024)} %get-tuple-element.13, f32[3072]{0:T(1024)} %get-tuple-element.68, ...), channel_id=1, replica_groups=mesh['dp'=16,'seq'=2] {'dp','seq'}, use_global_device_ids=true, to_apply=%region_21.22 | all-reduce | flops 9984 | bytes 79872 | tf_op jit(solution)/shard_map/psum | solution.py:235
  737.4 2.8 fusion.65
  740.2 1.6 convert_element_type.211
  741.8 1.6 transpose.56
  743.4 1.7 convert_element_type.209
  745.1 1.8 convert_element_type.213
  (172 shorter events, 14.9 us)
Async XLA Ops:
  7.2 7.8 %copy-start = (bf16[768,2304]{1,0:T(8,128)(2,1)S(1)}, bf16[768,2304]{1,0:T(8,128)(2,1)}, u32[]{:S(2)}) copy-start(bf16[768,2304]{1,0:T(8,128)(2,1)} %param.19) | copy-start | bytes 10616836
  7.2 55.0 %all-gather.5.cloned.1.call-start = ((), (), s32[]{:S(2)}) async-start(), calls=%async_computation.8 | async-start | bytes 2359296 | tf_op jit(solution)/shard_map/all_gather | solution.py:115
  8.7 3.1 copy-start.52
  8.7 4.9 copy-start.11
  8.8 5.5 copy-start.40
  8.8 6.2 copy-start.4
  10.2 6.9 copy-start.23
  11.7 3.2 copy-start.21
  13.7 1.3 copy-start.46
  14.9 2.3 copy-start.34
  14.9 2.3 copy-start.51
  17.2 3.1 copy-start.14
  27.9 3.3 copy-start.17
  32.1 2.5 copy-start.53
  32.2 59.4 %all-gather.3.cloned.1.call-start = ((), (), s32[]{:S(2)}) async-start(), calls=%async_computation.7 | async-start | bytes 2359296 | tf_op jit(solution)/shard_map/all_gather | solution.py:116
  34.6 167.1 %reduce-scatter.8.cloned.1.call-start = ((), (), s32[]{:S(2)}) async-start(), calls=%async_computation.9 | async-start | bytes 2359296 | tf_op jit(solution)/shard_map/reduce_scatter | solution.py:199
  94.2 11.2 %copy-start.5 = (bf16[1,512,768]{2,1,0:T(8,128)(2,1)S(1)}, bf16[1,512,768]{2,1,0:T(8,128)(2,1)}, u32[]{:S(2)}) copy-start(bf16[1,512,768]{2,1,0:T(8,128)(2,1)} %param.14) | copy-start | bytes 2359300
  94.2 11.2 %copy-start.16 = (bf16[768,768]{1,0:T(8,128)(2,1)S(1)}, bf16[768,768]{1,0:T(8,128)(2,1)}, u32[]{:S(2)}) copy-start(bf16[768,768]{1,0:T(8,128)(2,1)} %param.20) | copy-start | bytes 3538948
  105.3 2.0 copy-start.7
  107.4 17.3 %copy-start.2 = (f32[1,512,768]{2,1,0:T(8,128)}, f32[1,512,768]{2,1,0:T(8,128)S(1)}, u32[]{:S(2)}) copy-start(f32[1,512,768]{2,1,0:T(8,128)S(1)} %get-tuple-element.40) | copy-start | bytes 4718596
  107.4 0.7 copy-start.50
  107.4 6.3 slice-start.2
  107.7 16.9 %copy-start.41 = (f32[512]{0:T(512)}, f32[512]{0:T(512)S(1)}, u32[]{:S(2)}) copy-start(f32[512]{0:T(512)S(1)} %fusion.61) | copy-start | bytes 6148
  108.1 5.6 copy-start.15
  108.1 5.6 copy-start.29
  108.1 5.6 copy-start.37
  108.1 5.7 slice-start.3
  108.1 12.8 %slice-start = ((s8[4718592]{0:T(1024)(128)(4,1)}), s8[524288]{0:T(1024)(128)(4,1)S(1)}, s32[]{:S(2)}) async-start(s8[4718592]{0:T(1024)(128)(4,1)} %bitcast.158), calls=%async_computation.17 | async-start | bytes 1048576
  113.7 7.2 copy-start.54
  113.8 7.2 slice-start.1
  121.0 3.7 copy-start.55
  124.7 1.2 copy-start.8
  125.8 1.2 copy-start.9
  125.8 1.2 copy-start.43
  148.7 17.0 %copy-start.12 = (bf16[512,12,32]{0,2,1:T(8,128)(2,1)S(1)}, bf16[512,12,32]{0,2,1:T(8,128)(2,1)}, u32[]{:S(2)}) copy-start(bf16[512,12,32]{0,2,1:T(8,128)(2,1)} %get-tuple-element.48) | copy-start | bytes 1179652
  148.7 17.0 %copy-start.13 = (bf16[512,12,32]{0,2,1:T(8,128)(2,1)S(1)}, bf16[512,12,32]{0,2,1:T(8,128)(2,1)}, u32[]{:S(2)}) copy-start(bf16[512,12,32]{0,2,1:T(8,128)(2,1)} %get-tuple-element.49) | copy-start | bytes 1179652
  165.7 5.0 copy-start.1
  170.7 55.1 %reduce-scatter.10.cloned.1.call-start = ((), (), s32[]{:S(2)}) async-start(), calls=%async_computation.10 | async-start | bytes 2359296 | tf_op jit(solution)/shard_map/reduce_scatter | solution.py:205
  183.5 109.0 %reduce-scatter.14.cloned.1.call-start = ((), (), s32[]{:S(2)}) async-start(), calls=%async_computation.12 | async-start | bytes 2506752 | tf_op jit(solution)/shard_map/reduce_scatter | solution.py:242
  201.6 157.0 %reduce-scatter.20.cloned.1.call-start = ((), (), s32[]{:S(2)}) async-start(), calls=%async_computation.15 | async-start | bytes 2506752 | tf_op jit(solution)/shard_map/reduce_scatter | solution.py:245
  201.7 1.6 copy-start.10
  201.7 1.6 copy-start.18
  201.7 1.6 copy-start.20
  225.9 5.2 copy-start.22
  233.8 3.6 copy-start.26
  233.8 4.8 copy-start.3
  233.8 4.8 copy-start.6
  233.8 4.8 copy-start.24
  233.8 4.8 copy-start.30
  233.8 4.8 copy-start.35
  233.8 4.8 copy-start.38
  233.8 4.8 copy-start.44
  233.8 4.8 copy-start.45
  233.8 4.8 copy-start.49
  238.6 12.2 %copy-start.25 = (f32[768]{0:T(1024)S(1)}, f32[768]{0:T(1024)}, u32[]{:S(2)}) copy-start(f32[768]{0:T(1024)} %reduce_sum.236) | copy-start | bytes 9220
  238.6 12.7 %copy-start.48 = (f32[768]{0:T(1024)S(1)}, f32[768]{0:T(1024)}, u32[]{:S(2)}) copy-start(f32[768]{0:T(1024)} %get-tuple-element.15) | copy-start | bytes 9220
  257.4 194.4 %reduce-scatter.12.cloned.1.call-start = ((), (), s32[]{:S(2)}) async-start(), calls=%async_computation.11 | async-start | bytes 7520256 | tf_op jit(solution)/shard_map/reduce_scatter | solution.py:241
  264.8 302.5 %reduce-scatter.16.cloned.1.call-start = ((), (), s32[]{:S(2)}) async-start(), calls=%async_computation.13 | async-start | bytes 10027008 | tf_op jit(solution)/shard_map/reduce_scatter | solution.py:243
  274.3 0.7 copy-start.39
  274.3 408.2 %reduce-scatter.18.cloned.1.call-start = ((), (), s32[]{:S(2)}) async-start(), calls=%async_computation.14 | async-start | bytes 10027008 | tf_op jit(solution)/shard_map/reduce_scatter | solution.py:244
  285.7 454.6 %all-reduce.4.cloned.1.call-start = ((), (), s32[]{:S(2)}) async-start(), calls=%async_computation.16 | async-start | bytes 1916928 | tf_op jit(solution)/shard_map/psum | solution.py:248
  569.1 127.4 %copy-start.36 = (f32[768]{0:T(1024)S(1)}, f32[768]{0:T(1024)}, u32[]{:S(2)}) copy-start(f32[768]{0:T(1024)} %get-tuple-element.16) | copy-start | bytes 9220
  569.1 168.3 %copy-start.47 = (f32[128]{0:T(128)S(1)}, f32[128]{0:T(128)}, u32[]{:S(2)}) copy-start(f32[128]{0:T(128)} %copy-done.46) | copy-start | bytes 1540
  740.2 6.7 copy-start.19
  (6 other events, 4.1 us)
Sparse Core Ops, SparseCore 0:
  32.3 29.8 all-gather.4
  64.3 27.1 all-gather.2
  170.9 26.0 reduce-scatter.7
  199.7 26.0 reduce-scatter.9
  229.5 62.9 reduce-scatter.13
  296.6 61.9 reduce-scatter.19
  362.6 89.0 reduce-scatter.11
  456.4 110.8 reduce-scatter.15
  571.4 111.0 reduce-scatter.17
  686.3 39.1 all-reduce.3
where the time goes:
time: 763 us; the launch traced here: 755 us
  waiting for transfers between devices  440 us (58%)
  matrix products  145 us (19%)
  other arithmetic  77 us (10%)
  blocking collectives  50.4 us (7%)
  local copies, waits for them, and re-layouts  25.7 us (3%)
  between operations  16.2 us (2%)
    reduce_scatter x1, waiting for transfers between devices, per_device(): lax.psum_scatter(matrices[2], 'dp', scatter_dimension=0, tiled=True)  114 us
    reduce_scatter x1, waiting for transfers between devices, per_device(): lax.psum_scatter(matrices[3], 'dp', scatter_dimension=0, tiled=True)  113 us
    reduce_scatter x1, waiting for transfers between devices, per_device(): lax.psum_scatter(matrices[0], 'dp', scatter_dimension=0, tiled=True)  91.6 us
    reduce_scatter x1, waiting for transfers between devices, per_device(): lax.psum_scatter(matrices[4], 'dp', scatter_dimension=0, tiled=True)  64.6 us
    psum x1, blocking collectives, per_device(): lax.psum((first_gain_grad, second_gain_grad, up_bias_grad, down_bias_grad...  40.9 us
    dot_general x4, matrix products, outer_sum(): lax.dot_general(left, right, (((0,), (0,)), ((), ())), preferred_element_...  30.8 us
    all_gather x1, waiting for transfers between devices, per_device(): lax.all_gather(keys_low, 'seq', axis=1, tiled=True)  25.7 us
    reduce_scatter x1, waiting for transfers between devices, per_device(): lax.psum_scatter(d_values_all.reshape(rows_here, seq_length, model_width)...  20.6 us
  transfers between devices with their start and end apart: 10, of which 8 were waited for; matrix products, arithmetic and copies ran while one was open for 18% of the time, Pallas kernels for 0%

commit v1 on v0

--- a/solution.py
+++ b/solution.py
@@ -52,6 +52,113 @@
     return lax.dot_general(
         left, right, (((1,), (1,)), ((), ())), preferred_element_type=jnp.float32
     )
+
+
+def swap_halves(block):
+    count = lax.axis_size("dp") * lax.axis_size("seq")
+    target = {1: 2, 2: 1}
+    perm = [(i, i - i % 4 + target.get(i % 4, i % 4)) for i in range(count)]
+    return lax.ppermute(block, ("dp", "seq"), perm)
+
+
+def swap_bit(block, bit):
+    return lax.ppermute(block, "dp", [(i, i ^ bit) for i in range(lax.axis_size("dp"))])
+
+
+def swap_cores(block):
+    return swap_bit(block, 1)
+
+
+def swap_seq(block):
+    return lax.ppermute(block, "seq", [(0, 1), (1, 0)])
+
+
+def dp_bits():
+    bits, bit = [], 1
+    while bit < lax.axis_size("dp"):
+        bits.append(bit)
+        bit *= 2
+    return bits
+
+
+def pick(block, axis, index):
+    return lax.dynamic_index_in_dim(block, index, axis, keepdims=False)
+
+
+def scatter_sum(matrix, seq_first):
+    dp_size = lax.axis_size("dp")
+    dp_rank = lax.axis_index("dp")
+    seq_rank = lax.axis_index("seq")
+    rows, columns = matrix.shape
+    own = rows // dp_size
+    low = jnp.bfloat16
+    block = matrix.astype(low).reshape(dp_size, own, columns)
+
+    def by_bit(block, bit, done):
+        mine = (dp_rank // bit) % 2
+        count, rest, width = block.shape
+        inner = 1
+        low_bit = 1
+        while low_bit < bit:
+            if low_bit not in done:
+                inner *= 2
+            low_bit *= 2
+        split = block.reshape(count // (2 * inner), 2, inner, rest, width)
+        got = swap_bit(pick(split, 1, 1 - mine), bit)
+        kept = pick(split, 1, mine)
+        total = kept.astype(jnp.float32) + got.astype(jnp.float32)
+        return total.astype(low).reshape(count // 2, rest, width)
+
+    block = by_bit(block, 1, [])
+    done = [1]
+    if seq_first:
+        count, rest, width = block.shape
+        split = block.reshape(count, 2, rest // 2, width)
+        got = swap_seq(pick(split, 1, 1 - seq_rank))
+        total = pick(split, 1, seq_rank).astype(jnp.float32) + got.astype(jnp.float32)
+        block = total.astype(low)
+    for bit in dp_bits()[1:]:
+        block = by_bit(block, bit, done)
+        done.append(bit)
+    block = block[0]
+    got = swap_seq(block)
+    if seq_first:
+        first = jnp.where(seq_rank == 0, block, got)
+        second = jnp.where(seq_rank == 0, got, block)
+        return jnp.concatenate([first, second], axis=0).astype(jnp.float32)
+    return block.astype(jnp.float32) + got.astype(jnp.float32)
+
+
+def share_small(per_sequence, cond, summed):
+    dp_rank = lax.axis_index("dp")
+    seq_rank = lax.axis_index("seq")
+    sizes = [part.shape[0] for part in summed]
+    totals = jnp.concatenate(summed)
+    joined = jnp.concatenate([per_sequence[0], totals])
+    joined = joined + swap_cores(joined)
+    width = per_sequence.shape[1]
+    gathered = jnp.concatenate([joined[:width], cond[0]])[None]
+    totals = joined[width:]
+
+    def double(gathered, totals, mine, move):
+        count = gathered.shape[0]
+        sent = jnp.concatenate([gathered.reshape(-1), totals])
+        got = move(sent)
+        theirs = got[: gathered.size].reshape(gathered.shape)
+        first = jnp.where(mine == 0, gathered, theirs)
+        second = jnp.where(mine == 0, theirs, gathered)
+        return jnp.concatenate([first, second], axis=0), totals + got[gathered.size :]
+
+    gathered, totals = double(gathered, totals, seq_rank, swap_seq)
+    for bit in dp_bits()[1:]:
+        gathered, totals = double(
+            gathered, totals, (dp_rank // bit) % 2, lambda sent, bit=bit: swap_bit(sent, bit)
+        )
+    parts, start = [], 0
+    for size in sizes:
+        parts.append(totals[start : start + size])
+        start += size
+    return gathered[:, :width], gathered[:, width:], parts
 
 
 def per_device(
@@ -73,16 +180,19 @@
     rows_here, pos_here, model_width = tokens.shape
     head_count = H
     head_dim = HD
-    seq_rank = lax.axis_index("seq")
     seq_length = pos_here * lax.axis_size("seq")
     scale_factor = head_dim ** (-0.5)
     flat_rows = rows_here * pos_here
-    steps_count = step_table.shape[0]
-    picks = (time_index[:, None] == jnp.arange(steps_count, dtype=jnp.int32)[None, :]).astype(
-        jnp.float32
-    )
-    embedded = jnp.dot(picks, step_table, precision=highest)
-    cond, silu_back = jax.vjp(jax.nn.silu, embedded)
+    dp_rank = lax.axis_index("dp")
+    core = dp_rank % 2
+    own_cond, silu_back = jax.vjp(
+        jax.nn.silu, lax.dynamic_slice_in_dim(step_table, time_index[0], 1, axis=0)
+    )
+    tokens = swap_halves(tokens)
+    cotangent = swap_halves(cotangent)
+    time_index = swap_halves(time_index)
+    embedded = lax.dynamic_slice_in_dim(step_table, time_index[0], 1, axis=0)
+    cond = jax.nn.silu(embedded)
     ada_float = ada_weight.astype(jnp.float32)
     modulation = jnp.dot(cond, ada_float, precision=highest) + ada_bias.astype(jnp.float32)
     blocks = [
@@ -95,7 +205,7 @@
     projected = jnp.dot(normed_low, attn_qkv, preferred_element_type=jnp.float32).reshape(
         rows_here, pos_here, 3 * model_width
     )
-    positions = seq_rank * pos_here + jnp.arange(pos_here, dtype=jnp.int32)
+    positions = core * pos_here + jnp.arange(pos_here, dtype=jnp.int32)
     cosine, sine_table = tables(positions, head_dim)
 
     def turned(block):
@@ -111,10 +221,8 @@
     query_low = turned(projected[..., :model_width]).astype(jnp.bfloat16)
     keys_low = turned(projected[..., model_width : 2 * model_width]).astype(jnp.bfloat16)
     values_low = projected[..., 2 * model_width :].astype(jnp.bfloat16)
-    all_keys, all_values = (
-        lax.all_gather(keys_low, "seq", axis=1, tiled=True),
-        lax.all_gather(values_low, "seq", axis=1, tiled=True),
-    )
+    all_keys = jnp.concatenate([keys_low, swap_cores(keys_low)], axis=1)
+    all_values = jnp.concatenate([values_low, swap_cores(values_low)], axis=1)
     query_heads = query_low.reshape(rows_here, pos_here, head_count, head_dim)
 
     def scored(key_block):
@@ -195,20 +303,13 @@
         jnp.einsum("bhqk,bqhd->bkhd", d_scores, query_heads, preferred_element_type=jnp.float32)
         * scale_factor
     )
-    d_keys_own, d_values_own = (
-        lax.psum_scatter(
-            d_keys_all.reshape(rows_here, seq_length, model_width).astype(jnp.bfloat16),
-            "seq",
-            scatter_dimension=1,
-            tiled=True,
-        ).astype(jnp.float32),
-        lax.psum_scatter(
-            d_values_all.reshape(rows_here, seq_length, model_width).astype(jnp.bfloat16),
-            "seq",
-            scatter_dimension=1,
-            tiled=True,
-        ).astype(jnp.float32),
-    )
+    def from_pair(block):
+        block = block.reshape(rows_here, seq_length, model_width)
+        theirs = swap_cores(block[:, pos_here:].astype(jnp.bfloat16))
+        return block[:, :pos_here] + theirs.astype(jnp.float32)
+
+    d_keys_own = from_pair(d_keys_all)
+    d_values_own = from_pair(d_values_all)
     d_projected = (
         jnp.concatenate(
             [
@@ -228,43 +329,41 @@
     d_modulation = jnp.concatenate(
         [d_shift1[:, 0], d_scale1[:, 0], d_gate1, d_shift2[:, 0], d_scale2[:, 0], d_gate2], -1
     )
-    ada_turned = jnp.dot(d_modulation.T, cond, precision=highest)
-    ada_bias_grad = jnp.sum(d_modulation, axis=0)
-    d_mod_total = lax.psum(d_modulation, "seq")
-    (cond_grad,) = silu_back(jnp.dot(d_mod_total, ada_float.T, precision=highest))
-    small_total = lax.psum(
-        (first_gain_grad, second_gain_grad, up_bias_grad, down_bias_grad, ada_bias_grad),
-        ("dp", "seq"),
-    )
-    matrices = (attn_qkv_grad, attn_out_grad, mlp_up_grad, mlp_down_grad, ada_turned)
-    row_parts = (
-        lax.psum_scatter(matrices[0], "dp", scatter_dimension=0, tiled=True),
-        lax.psum_scatter(matrices[1], "dp", scatter_dimension=0, tiled=True),
-        lax.psum_scatter(matrices[2], "dp", scatter_dimension=0, tiled=True),
-        lax.psum_scatter(matrices[3], "dp", scatter_dimension=0, tiled=True),
-        lax.psum_scatter(matrices[4], "dp", scatter_dimension=0, tiled=True),
-    )
-    row_total = (
-        lax.psum(row_parts[0].astype(jnp.bfloat16), "seq").astype(jnp.float32),
-        lax.psum(row_parts[1].astype(jnp.bfloat16), "seq").astype(jnp.float32),
-        lax.psum(row_parts[2].astype(jnp.bfloat16), "seq").astype(jnp.float32),
-        lax.psum(row_parts[3].astype(jnp.bfloat16), "seq").astype(jnp.float32),
-        lax.psum(row_parts[4].astype(jnp.bfloat16), "seq").astype(jnp.float32),
+    d_mod_all, cond_all, sums = share_small(
+        d_modulation,
+        cond,
+        (first_gain_grad, second_gain_grad, up_bias_grad, down_bias_grad),
+    )
+    ada_bias_grad = jnp.sum(d_mod_all, axis=0)
+    own_columns = d_mod_all.shape[1] // lax.axis_size("dp")
+    mine = lax.dynamic_slice_in_dim(d_mod_all, dp_rank * own_columns, own_columns, axis=1)
+    ada_weight_grad = lax.dot_general(
+        cond_all, mine, (((0,), (0,)), ((), ())), precision=highest
+    )
+    d_mod_own = lax.dynamic_slice_in_dim(d_mod_all, dp_rank, 1, axis=0)
+    (cond_grad,) = silu_back(jnp.dot(d_mod_own, ada_float.T, precision=highest))
+    half = attn_qkv_grad.shape[1] // 2
+    qkv_rows = jnp.concatenate(
+        [
+            scatter_sum(attn_qkv_grad[:, :half], False),
+            scatter_sum(attn_qkv_grad[:, half:], True),
+        ],
+        axis=1,
     )
     return (
-        mixed,
-        tokens_grad,
+        swap_halves(mixed),
+        swap_halves(tokens_grad.astype(jnp.bfloat16)).astype(jnp.float32),
         cond_grad,
-        small_total[0],
-        row_total[0],
-        row_total[1],
-        small_total[1],
-        row_total[2],
-        small_total[2],
-        row_total[3],
-        small_total[3],
-        row_total[4].T,
-        small_total[4],
+        sums[0],
+        qkv_rows,
+        scatter_sum(attn_out_grad, True),
+        sums[1],
+        scatter_sum(mlp_up_grad, False),
+        sums[2],
+        scatter_sum(mlp_down_grad, True),
+        sums[3],
+        ada_weight_grad,
+        ada_bias_grad,
     )
 
 

time: 763 us -> 468 us (0.61)
  waiting for transfers between devices: 440 us -> 93 us
  starting transfers between devices: 0.88 us -> 68.7 us
  blocking collectives: 50.4 us -> 0 us
  local copies, waits for them, and re-layouts: 25.7 us -> 57.6 us
  other arithmetic: 77 us -> 94.6 us
  between operations: 16.2 us -> 4.58 us
    reduce_scatter x7 -> x0, waiting for transfers between devices: 411 us -> none  [the longest x1 114 us: per_device(): lax.psum_scatter(matrices[2], 'dp', scatter_dimension=0, tiled=True)]
    ppermute x0 -> x42, waiting for transfers between devices: none -> 93 us  [the longest x28 55.3 us: swap_bit(): lax.ppermute(block, 'dp', [(i, i ^ bit) for i in range(lax.axis_size('dp'...]
    ppermute x0 -> x42, starting transfers between devices: none -> 68.7 us  [the longest x5 32.4 us: swap_halves(): return lax.ppermute(block, ('dp', 'seq'), perm)]
    psum x2 -> x0, blocking collectives: 50.4 us -> none  [the longest x1 40.9 us: per_device(): lax.psum((first_gain_grad, second_gain_grad, up_bias_grad, down_bias_grad...]
    all_gather x2 -> x0, waiting for transfers between devices: 28.7 us -> none  [the longest x1 25.7 us: per_device(): lax.all_gather(keys_low, 'seq', axis=1, tiled=True)]
    dot_general x4, matrix products: 30.8 us -> 18.6 us  [outer_sum(): lax.dot_general(left, right, (((0,), (0,)), ((), ())), preferred_element_...]
    squeeze x0 -> x23, local copies, waits for them, and re-layouts: none -> 10.8 us  [pick(): return lax.dynamic_index_in_dim(block, index, axis, keepdims=False)]
    unnamed x125 -> x142, local copies, waits for them, and re-layouts: 8.44 us -> 17.9 us
  transfers between devices with their start and end apart: 10 -> 42, of which waited for: 8 -> 19; matrix products, arithmetic and copies ran while one was open for 18% -> 30% of each run, Pallas kernels for 0% -> 0%
where the time goes in v1:
time: 468 us; the launch traced here: 460 us
  matrix products  141 us (30%)
  other arithmetic  94.6 us (20%)
  waiting for transfers between devices  93 us (20%)
  starting transfers between devices  68.7 us (15%)
  local copies, waits for them, and re-layouts  57.6 us (12%)
    ppermute x28, waiting for transfers between devices, swap_bit(): lax.ppermute(block, 'dp', [(i, i ^ bit) for i in range(lax.axis_size('dp'...  55.3 us
    ppermute x9, waiting for transfers between devices, swap_seq(): return lax.ppermute(block, 'seq', [(0, 1), (1, 0)])  37.7 us
    ppermute x5, starting transfers between devices, swap_halves(): return lax.ppermute(block, ('dp', 'seq'), perm)  32.4 us
    ppermute x28, starting transfers between devices, swap_bit(): lax.ppermute(block, 'dp', [(i, i ^ bit) for i in range(lax.axis_size('dp'...  27.3 us
    convert_element_type x1, other arithmetic, per_device(): d_scores = (probs * (d_probs - delta_sum)).astype(jnp.bfloat16)  21.9 us
    dot_general x4, matrix products, back_mult(): lax.dot_general(left, right, (((1,), (1,)), ((), ())), preferred_element_...  20.7 us
    dot_general x4, matrix products, outer_sum(): lax.dot_general(left, right, (((0,), (0,)), ((), ())), preferred_element_...  18.6 us
    unnamed x142, local copies, waits for them, and re-layouts  17.9 us
  transfers between devices with their start and end apart: 42, of which 19 were waited for; matrix products, arithmetic and copies ran while one was open for 30% of the time, Pallas kernels for 0%

profile of v1, /device:TPU:0, one launch (start us, length us, event | category | flops | bytes accessed | tf_op | source)
XLA Modules:
  0.0 459.9 jit_solution(4331057413049158133)
XLA Ops:
  0.7 2.3 collective-permute-start.1
  2.9 7.4 %collective-permute-start = (bf16[1,512,768]{2,1,0:T(8,128)(2,1)}, bf16[1,512,768]{2,1,0:T(8,128)(2,1)}, u32[]{:S(2)}, u32[]{:S(2)}) collective-permute-start(bf16[1,512,768]{2,1,0:T(8,128)(2,1)} %param.14), channel_id=1, source_target_pairs={{0,0},{1,2},{2,1},{3,3},{4,4},{5,6},{6,5},{7,7},{8,8},{9,10},{10,9... | collective-permute-start | bytes 2359304 | tf_op jit(solution)/shard_map/ppermute | solution.py:61
  10.4 7.4 %collective-permute-start.5 = (bf16[1,512,768]{2,1,0:T(8,128)(2,1)}, bf16[1,512,768]{2,1,0:T(8,128)(2,1)}, u32[]{:S(2)}, u32[]{:S(2)}) collective-permute-start(bf16[1,512,768]{2,1,0:T(8,128)(2,1)} %param.15), channel_id=1, source_target_pairs={{0,0},{1,2},{2,1},{3,3},{4,4},{5,6},{6,5},{7,7},{8,8},{9,10},{10,9... | collective-permute-start | bytes 2359304 | tf_op jit(solution)/shard_map/ppermute | solution.py:61
  21.4 1.9 convolution_reduce_fusion
  27.5 3.3 convolution_bitcast_fusion
  31.8 1.9 fusion.115
  33.7 3.0 copy.59
  45.6 3.1 copy.58
  48.7 1.9 convert_reduce_fusion.2
  50.6 2.5 fusion.64
  53.1 2.6 pad_maximum_fusion.1
  55.7 3.1 copy.57
  58.8 13.4 %multiply_reduce_fusion.1 = (f32[12,512]{1,0:T(8,128)S(1)}, f32[12,512,1024]{2,1,0:T(8,128)}) fusion(bf16[1,512,12,64]{1,3,2,0:T(8,128)(2,1)} %bitcast.11, bf16[1,512,12,64]{1,3,2,0:T(8,128)(2,1)} %maximum_convert_fusion, bf16[512,12,32]{0,2,1:T(8,128)(2,1)} %get-tuple-element.43, bf16[512,12,32]{0,2,1:T(8,128)(2,1)} %get-tuple-element.42), kind=kOutput, calls=%fused_computation.4 | convolution fusion | flops 822601728 | bytes 27549696 | tf_op jit(solution)/shard_map/bqhd,bkhd->bhqk/dot_general | solution.py:231
  72.2 11.1 %exponential_reduce_fusion = f32[12,512]{1,0:T(8,128)S(1)} fusion(f32[12,512,1024]{2,1,0:T(8,128)} %get-tuple-element.70, f32[12,512]{1,0:T(8,128)S(1)} %get-tuple-element.69), kind=kLoop, calls=%fused_computation.3 | loop fusion | flops 18868224 | bytes 25214976 | tf_op jit(solution)/shard_map/reduce_sum | solution.py:239
  83.3 10.6 %fusion.40 = bf16[12,64,512]{2,1,0:T(8,128)(2,1)S(1)} fusion(bf16[1024,12,64]{0,2,1:T(8,128)(2,1)S(1)} %bitcast.271, f32[12,512,1024]{2,1,0:T(8,128)} %get-tuple-element.70, f32[12,512]{1,0:T(8,128)S(1)} %log_add_fusion), kind=kOutput, calls=%fused_computation.89 | convolution fusion | flops 824573952 | bytes 27549696 | tf_op jit(solution)/shard_map/bhqk,bkhd->bqhd/dot_general | solution.py:243
  94.0 3.4 fusion.114
  98.2 5.5 %fusion.108 = f32[512,3072]{1,0:T(8,128)S(1)} fusion(bf16[768,3072]{1,0:T(8,128)(2,1)} %param.22, f32[1,512,768]{2,1,0:T(8,128)S(1)} %get-tuple-element.32, f32[768]{0:T(1024)S(1)} %copy-done.55, f32[768]{0:T(1024)S(1)} %copy-done.47, f32[768]{0:T(1024)S(1)} %copy-done.39, f32[512]{0:T(512)S(1)} %fusion.89, f32[512]{0:T(512)S(1)} %broadcast_multiply_fusion), kind=kOutput, calls=%fused_computation.265 | convolution fusion | flops 2418278400 | bytes 12596224 | tf_op jit(solution)/shard_map/dot_general | solution.py:253
  103.8 9.2 %convert_reduce_fusion = (f32[3072]{0:T(1024)}, bf16[512,3072]{1,0:T(8,128)(2,1)S(1)}) fusion(f32[512,3072]{1,0:T(8,128)S(1)} %fusion.108, f32[3072]{0:T(1024)S(1)} %copy-done.48, bf16[3072,768]{1,0:T(8,128)(2,1)S(1)} %bitcast.328, bf16[1,512,768]{2,1,0:T(8,128)(2,1)} %collective-permute-done.5, f32[768]{0:T(1024)S(1)} %copy-done.43), kind=kOutput, calls=%fused_computation.15 | convolution fusion | flops 2453271552 | bytes 14969856 | tf_op jit(solution)/shard_map/dot_general | solution.py:52
  113.1 3.6 fusion.35
  116.7 4.7 %convolution_convert_fusion.1 = bf16[768,3072]{1,0:T(8,128)(2,1)} fusion(bf16[512,3072]{1,0:T(8,128)(2,1)S(1)} %get-tuple-element.78, f32[1,512,768]{2,1,0:T(8,128)S(1)} %get-tuple-element.32, f32[768]{0:T(1024)S(1)} %copy-done.55, f32[768]{0:T(1024)S(1)} %copy-done.47, f32[768]{0:T(1024)S(1)} %copy-done.39, f32[512]{0:T(512)S(1)} %fusion.89, ...), kind=kOutput, calls=%fused_computation.18 | convolution fusion | flops 2420637696 | bytes 9450496 | tf_op jit(solution)/shard_map/dot_general | solution.py:46
  123.4 2.9 convolution_convert_fusion.4
  126.3 2.3 copy.60
  128.6 12.5 %fusion.16 = f32[12,64,1024]{2,1,0:T(8,128)} fusion(bf16[512,12,64]{0,2,1:T(8,128)(2,1)} %bitcast.284, f32[12,512,1024]{2,1,0:T(8,128)} %get-tuple-element.70, f32[12,512]{1,0:T(8,128)} %copy-done.21), kind=kOutput, calls=%fused_computation.45 | convolution fusion | flops 824180736 | bytes 29122560 | tf_op jit(solution)/shard_map/bhqk,bqhd->bkhd/dot_general | solution.py:295
  141.1 17.5 %multiply_reduce_fusion = (f32[12,512]{1,0:T(8,128)}, f32[12,512,1024]{2,1,0:T(8,128)}) fusion(f32[12,512,1024]{2,1,0:T(8,128)} %get-tuple-element.70, f32[12,512]{1,0:T(8,128)} %copy-done.21, bf16[512,12,64]{0,2,1:T(8,128)(2,1)} %bitcast.285, bf16[1024,12,64]{0,2,1:T(8,128)(2,1)} %bitcast.270), kind=kOutput, calls=%fused_computation.1 | convolution fusion | flops 830466048 | bytes 52740096 | tf_op jit(solution)/shard_map/bqhd,bkhd->bhqk/dot_general | solution.py:290
  158.6 21.9 %multiply_convert_fusion = bf16[12,512,1024]{2,1,0:T(8,128)(2,1)} fusion(f32[12,512,1024]{2,1,0:T(8,128)} %get-tuple-element.74, f32[12,512,1024]{2,1,0:T(8,128)} %get-tuple-element.70, f32[12,512]{1,0:T(8,128)} %get-tuple-element.73, f32[12,512]{1,0:T(8,128)} %copy-done.21), kind=kLoop, calls=%fused_computation | loop fusion | flops 31457280 | bytes 62963712 | tf_op jit(solution)/shard_map/convert_element_type | solution.py:294
  180.5 10.3 %multiply_bitcast_fusion = f32[1,512,12,64]{1,3,2,0:T(8,128)} fusion(bf16[12,512,1024]{2,1,0:T(8,128)(2,1)} %multiply_convert_fusion, bf16[1,512,12,64]{1,3,2,0:T(8,128)(2,1)} %bitcast.11, bf16[1,512,12,64]{1,3,2,0:T(8,128)(2,1)} %maximum_convert_fusion), kind=kOutput, calls=%fused_computation.84 | convolution fusion | flops 808845312 | bytes 15728640 | tf_op jit(solution)/shard_map/bhqk,bkhd->bqhd/dot_general | solution.py:299
  190.8 8.6 %convolution_multiply_fusion = f32[12,64,1024]{2,1,0:T(8,128)} fusion(bf16[12,512,1024]{2,1,0:T(8,128)(2,1)} %multiply_convert_fusion, bf16[512,12,32]{0,2,1:T(8,128)(2,1)S(1)} %copy-done.14, bf16[512,12,32]{0,2,1:T(8,128)(2,1)S(1)} %copy-done.13), kind=kOutput, calls=%fused_computation.44 | convolution fusion | flops 807665664 | bytes 16515072 | tf_op jit(solution)/shard_map/bhqk,bqhd->bkhd/dot_general | solution.py:303
  199.3 2.1 reduce_sum.241
  201.5 2.8 convolution_convert_fusion.3
  204.4 3.5 dynamic-slice_bitcast_fusion.1
  209.4 7.0 %convolution_convert_fusion = bf16[3072,768]{1,0:T(8,128)(2,1)S(1)} fusion(bf16[1,512,768]{2,1,0:T(8,128)(2,1)} %collective-permute-done.5, f32[768]{0:T(1024)S(1)} %copy-done.44, f32[512,3072]{1,0:T(8,128)} %copy-done.59, f32[3072]{0:T(1024)S(1)} %copy-done.49), kind=kOutput, calls=%fused_computation.17 | convolution fusion | flops 2435186688 | bytes 11811840 | tf_op jit(solution)/shard_map/dot_general | solution.py:46
  220.2 2.3 collective-permute-start.26
  224.7 4.9 %fusion.31 = (f32[512]{0:T(512)S(1)}, f32[512,768]{1,0:T(8,128)}) fusion(bf16[1,512,768]{2,1,0:T(8,128)(2,1)} %collective-permute-done, f32[768]{0:T(1024)S(1)} %convert_element_type.554, f32[768]{0:T(1024)S(1)} %copy-done.41, f32[512]{0:T(512)S(1)} %broadcast_multiply_fusion.1, bf16[768,2304]{1,0:T(8,128)(2,1)S(1)} %copy-done, ...), kind=kOutput, calls=%fused_computation.60 | convolution fusion | flops 1821376000 | bytes 8267776 | tf_op jit(solution)/shard_map/dot_general | solution.py:52
  231.9 3.4 fusion.29
  236.5 11.1 %fusion.33 = (f32[768]{0:T(1024)S(1)}, f32[768]{0:T(1024)S(1)}, bf16[1,512,768]{2,1,0:T(8,128)(2,1)}, bf16[1,512,768]{2,1,0:T(8,128)(2,1)}) fusion(bf16[1,512,768]{2,1,0:T(8,128)(2,1)} %collective-permute-done.5, f32[768]{0:T(1024)S(1)} %copy-done.53, f32[512,768]{1,0:T(8,128)} %get-tuple-element.71, f32[1,512,768]{2,1,0:T(8,128)} %copy-done.18, ...), kind=kOutput, calls=%fused_computation.62 | convolution fusion | flops 2440296960 | bytes 20488192 | tf_op jit(solution)/shard_map/dot_general | solution.py:259
  258.0 4.2 convolution_convert_fusion.2
  262.5 7.7 %collective-permute-start.8 = (bf16[1,512,768]{2,1,0:T(8,128)(2,1)}, bf16[1,512,768]{2,1,0:T(8,128)(2,1)}, u32[]{:S(2)}, u32[]{:S(2)}) collective-permute-start(bf16[1,512,768]{2,1,0:T(8,128)(2,1)} %get-tuple-element.37), channel_id=1, source_target_pairs={{0,0},{1,2},{2,1},{3,3},{4,4},{5,6},{6,5},{7,7},{8,8},{9,10},{10,9... | collective-permute-start | bytes 2359304 | tf_op jit(solution)/shard_map/ppermute | solution.py:61
  270.2 7.6 %collective-permute-start.4 = (bf16[1,512,768]{2,1,0:T(8,128)(2,1)}, bf16[1,512,768]{2,1,0:T(8,128)(2,1)}, u32[]{:S(2)}, u32[]{:S(2)}) collective-permute-start(bf16[1,512,768]{2,1,0:T(8,128)(2,1)} %get-tuple-element.46), channel_id=1, source_target_pairs={{0,0},{1,2},{2,1},{3,3},{4,4},{5,6},{6,5},{7,7},{8,8},{9,10},{10,9... | collective-permute-start | bytes 2359304 | tf_op jit(solution)/shard_map/ppermute | solution.py:61
  280.0 6.0 %collective-permute-done.10 = f32[10112]{0:T(1024)S(1)} collective-permute-done((f32[10112]{0:T(1024)S(1)}, f32[10112]{0:T(1024)S(1)}, u32[]{:S(2)}, u32[]{:S(2)}) %collective-permute-start.10) | collective-permute-done | bytes 40480 | tf_op jit(solution)/shard_map/ppermute | solution.py:73
  290.1 1.8 collective-permute-start.11
  291.9 1.8 fusion.61
  303.2 1.9 collective-permute-start.12
  314.4 1.9 collective-permute-start.28
  317.0 1.9 collective-permute-done.28
  320.1 2.8 collective-permute-start.29
  328.3 2.3 collective-permute-done.30
  330.7 2.3 collective-permute-start.13
  333.6 5.3 %collective-permute-done.13 = f32[43264]{0:T(1024)S(1)} collective-permute-done((f32[43264]{0:T(1024)S(1)}, f32[43264]{0:T(1024)S(1)}, u32[]{:S(2)}, u32[]{:S(2)}) %collective-permute-start.13) | collective-permute-done | bytes 173088 | tf_op jit(solution)/shard_map/ppermute | solution.py:65
  345.7 2.8 fusion.91
  349.7 2.4 convert_element_type.579
  357.4 8.9 %collective-permute-done.15 = bf16[4,1,48,1152]{3,2,0,1:T(8,128)(2,1)S(1)} collective-permute-done((bf16[4,1,48,1152]{3,2,0,1:T(8,128)(2,1)S(1)}, bf16[4,1,48,1152]{3,2,0,1:T(8,128)(2,1)S(1)}, u32[]{:S(2)}, u32[]{:S(2)}) %collective-permute-start.15) | collective-permute-done | bytes 442400 | tf_op jit(solution)/shard_map/ppermute | solution.py:65
  366.9 2.2 collective-permute-done.20
  369.8 3.8 collective-permute-done.16
  373.7 2.0 collective-permute-start.17
  377.6 3.3 fusion.9
  385.5 3.4 collective-permute-done.23
  391.1 21.7 %collective-permute-done.24 = bf16[24,1152]{1,0:T(8,128)(2,1)S(1)} collective-permute-done((bf16[24,1152]{1,0:T(8,128)(2,1)S(1)}, bf16[24,1152]{1,0:T(8,128)(2,1)S(1)}, u32[]{:S(2)}, u32[]{:S(2)}) %collective-permute-start.24) | collective-permute-done | bytes 55328 | tf_op jit(solution)/shard_map/ppermute | solution.py:73
  415.7 8.5 %collective-permute-done.38 = bf16[4,1,96,768]{3,2,0,1:T(8,128)(2,1)S(1)} collective-permute-done((bf16[4,1,96,768]{3,2,0,1:T(8,128)(2,1)S(1)}, bf16[4,1,96,768]{3,2,0,1:T(8,128)(2,1)S(1)}, u32[]{:S(2)}, u32[]{:S(2)}) %collective-permute-start.38) | collective-permute-done | bytes 589856 | tf_op jit(solution)/shard_map/ppermute | solution.py:65
  425.1 6.8 %collective-permute-done.33 = bf16[2,1,48,3072]{3,2,0,1:T(8,128)(2,1)S(1)} collective-permute-done((bf16[2,1,48,3072]{3,2,0,1:T(8,128)(2,1)S(1)}, bf16[2,1,48,3072]{3,2,0,1:T(8,128)(2,1)S(1)}, u32[]{:S(2)}, u32[]{:S(2)}) %collective-permute-start.33) | collective-permute-done | bytes 589856 | tf_op jit(solution)/shard_map/ppermute | solution.py:65
  432.2 2.9 collective-permute-done.39
  437.2 10.9 %collective-permute-done.40 = bf16[1,1,96,768]{3,2,0,1:T(8,128)(2,1)S(1)} collective-permute-done((bf16[1,1,96,768]{3,2,0,1:T(8,128)(2,1)S(1)}, bf16[1,1,96,768]{3,2,0,1:T(8,128)(2,1)S(1)}, u32[]{:S(2)}, u32[]{:S(2)}) %collective-permute-start.40) | collective-permute-done | bytes 147488 | tf_op jit(solution)/shard_map/ppermute | solution.py:65
  450.3 3.3 collective-permute-done.41
  454.5 2.3 collective-permute-done.35
  457.6 2.1 copy.85
  (325 shorter events, 105.7 us)
Async XLA Ops:
  0.6 26.8 %copy-start = (bf16[768,2304]{1,0:T(8,128)(2,1)S(1)}, bf16[768,2304]{1,0:T(8,128)(2,1)}, u32[]{:S(2)}) copy-start(bf16[768,2304]{1,0:T(8,128)(2,1)} %param.19) | copy-start | bytes 10616836
  0.7 18.9 %collective-permute-start.1 = (s32[1]{0:T(128)}, s32[1]{0:T(128)}, u32[]{:S(2)}, u32[]{:S(2)}) collective-permute-start(s32[1]{0:T(128)} %param.16), channel_id=1, source_target_pairs={{0,0},{1,2},{2,1},{3,3},{4,4},{5,6},{6,5},{7,7},{8,8},{9,10},{10,9... | collective-permute-start | bytes 20 | tf_op jit(solution)/shard_map/ppermute | solution.py:61
  2.9 21.7 %collective-permute-start = (bf16[1,512,768]{2,1,0:T(8,128)(2,1)}, bf16[1,512,768]{2,1,0:T(8,128)(2,1)}, u32[]{:S(2)}, u32[]{:S(2)}) collective-permute-start(bf16[1,512,768]{2,1,0:T(8,128)(2,1)} %param.14), channel_id=1, source_target_pairs={{0,0},{1,2},{2,1},{3,3},{4,4},{5,6},{6,5},{7,7},{8,8},{9,10},{10,9... | collective-permute-start | bytes 2359304 | tf_op jit(solution)/shard_map/ppermute | solution.py:61
  10.4 38.3 %collective-permute-start.5 = (bf16[1,512,768]{2,1,0:T(8,128)(2,1)}, bf16[1,512,768]{2,1,0:T(8,128)(2,1)}, u32[]{:S(2)}, u32[]{:S(2)}) collective-permute-start(bf16[1,512,768]{2,1,0:T(8,128)(2,1)} %param.15), channel_id=1, source_target_pairs={{0,0},{1,2},{2,1},{3,3},{4,4},{5,6},{6,5},{7,7},{8,8},{9,10},{10,9... | collective-permute-start | bytes 2359304 | tf_op jit(solution)/shard_map/ppermute | solution.py:61
  24.6 6.2 %copy-start.54 = (f32[768]{0:T(1024)}, f32[768]{0:T(1024)S(1)}, u32[]{:S(2)}) copy-start(f32[768]{0:T(1024)S(1)} %get-tuple-element.24) | copy-start | bytes 9220
  31.8 21.3 %collective-permute-start.2 = (bf16[1,512,768]{2,1,0:T(8,128)(2,1)}, bf16[1,512,768]{2,1,0:T(8,128)(2,1)}, u32[]{:S(2)}, u32[]{:S(2)}) collective-permute-start(bf16[1,512,768]{2,1,0:T(8,128)(2,1)} %slice.258), channel_id=1, source_target_pairs={{0,2},{2,0},{4,6},{6,4},{8,10},{10,8},{12,14},{14,12},{16,18},{18,... | collective-permute-start | bytes 2359304 | tf_op jit(solution)/shard_map/ppermute | solution.py:65
  39.4 19.4 %collective-permute-start.3 = (bf16[1,512,768]{1,2,0:T(8,128)(2,1)}, bf16[1,512,768]{1,2,0:T(8,128)(2,1)}, u32[]{:S(2)}, u32[]{:S(2)}) collective-permute-start(bf16[1,512,768]{1,2,0:T(8,128)(2,1)} %bitcast.10), channel_id=1, source_target_pairs={{0,2},{2,0},{4,6},{6,4},{8,10},{10,8},{12,14},{14,12},{16,18},{18,... | collective-permute-start | bytes 2359304 | tf_op jit(solution)/shard_map/ppermute | solution.py:65
  72.2 11.1 %copy-start.1 = (bf16[1,1024,768]{1,2,0:T(8,128)(2,1)S(1)}, bf16[1,1024,768]{1,2,0:T(8,128)(2,1)}, u32[]{:S(2)}) copy-start(bf16[1,1024,768]{1,2,0:T(8,128)(2,1)} %copy.57) | copy-start | bytes 4718596
  83.3 10.7 %copy-start.21 = (f32[12,512]{1,0:T(8,128)}, f32[12,512]{1,0:T(8,128)S(1)}, u32[]{:S(2)}) copy-start(f32[12,512]{1,0:T(8,128)S(1)} %log_add_fusion) | copy-start | bytes 73732
  83.3 10.7 %copy-start.19 = (bf16[768,768]{1,0:T(8,128)(2,1)S(1)}, bf16[768,768]{1,0:T(8,128)(2,1)}, u32[]{:S(2)}) copy-start(bf16[768,768]{1,0:T(8,128)(2,1)} %param.20) | copy-start | bytes 3538948
  83.3 10.7 %copy-start.46 = (f32[768]{0:T(1024)S(1)}, f32[768]{0:T(1024)}, u32[]{:S(2)}) copy-start(f32[768]{0:T(1024)} %get-tuple-element.26) | copy-start | bytes 9220
  97.4 24.0 %copy-start.2 = (f32[1,512,768]{2,1,0:T(8,128)}, f32[1,512,768]{2,1,0:T(8,128)S(1)}, u32[]{:S(2)}) copy-start(f32[1,512,768]{2,1,0:T(8,128)S(1)} %get-tuple-element.32) | copy-start | bytes 4718596
  97.4 6.3 %slice-start.4 = ((s8[4718592]{0:T(1024)(128)(4,1)}), s8[4194304]{0:T(1024)(128)(4,1)S(1)}, s32[]{:S(2)}) async-start(s8[4718592]{0:T(1024)(128)(4,1)} %bitcast.327), calls=%async_computation.4 | async-start | bytes 8388608
  98.2 14.9 %slice-start.2 = ((s8[4718592]{0:T(1024)(128)(4,1)}), s8[4194304]{0:T(1024)(128)(4,1)S(1)}, s32[]{:S(2)}) async-start(s8[4718592]{0:T(1024)(128)(4,1)} %bitcast.325), calls=%async_computation.2 | async-start | bytes 8388608
  103.8 9.3 %copy-start.59 = (f32[512,3072]{1,0:T(8,128)}, f32[512,3072]{1,0:T(8,128)S(1)}, u32[]{:S(2)}) copy-start(f32[512,3072]{1,0:T(8,128)S(1)} %fusion.108) | copy-start | bytes 18874372
  103.8 9.3 %slice-start.3 = ((s8[4718592]{0:T(1024)(128)(4,1)}), s8[524288]{0:T(1024)(128)(4,1)S(1)}, s32[]{:S(2)}) async-start(s8[4718592]{0:T(1024)(128)(4,1)} %bitcast.325), calls=%async_computation.3 | async-start | bytes 1048576
  180.5 10.3 %copy-start.13 = (bf16[512,12,32]{0,2,1:T(8,128)(2,1)S(1)}, bf16[512,12,32]{0,2,1:T(8,128)(2,1)}, u32[]{:S(2)}) copy-start(bf16[512,12,32]{0,2,1:T(8,128)(2,1)} %get-tuple-element.42) | copy-start | bytes 1179652
  180.5 10.3 %copy-start.14 = (bf16[512,12,32]{0,2,1:T(8,128)(2,1)S(1)}, bf16[512,12,32]{0,2,1:T(8,128)(2,1)}, u32[]{:S(2)}) copy-start(bf16[512,12,32]{0,2,1:T(8,128)(2,1)} %get-tuple-element.43) | copy-start | bytes 1179652
  204.3 14.9 %collective-permute-start.25 = (bf16[8,1,48,768]{3,2,0,1:T(8,128)(2,1)S(1)}, bf16[8,1,48,768]{3,2,0,1:T(8,128)(2,1)S(1)}, u32[]{:S(2)}, u32[]{:S(2)}) collective-permute-start(bf16[8,1,48,768]{3,2,0,1:T(8,128)(2,1)S(1)} %dynamic-slice_bitcast_fusion.8), channel_id=1, source_target_pairs={{0,2},{2,0},{4,6},{6,4},{8,10},{10,8},{12,14},{14,12},{16,18},{18,... | collective-permute-start | bytes 1769480 | tf_op jit(solution)/shard_map/ppermute | solution.py:65
  207.9 169.8 %collective-permute-start.31 = (bf16[8,1,48,3072]{3,2,0,1:T(8,128)(2,1)}, bf16[8,1,48,3072]{3,2,0,1:T(8,128)(2,1)}, u32[]{:S(2)}, u32[]{:S(2)}) collective-permute-start(bf16[8,1,48,3072]{3,2,0,1:T(8,128)(2,1)} %dynamic-slice_bitcast_fusion.1), channel_id=1, source_target_pairs={{0,2},{2,0},{4,6},{6,4},{8,10},{10,8},{12,14},{14,12},{16,18},{18,... | collective-permute-start | bytes 7077896 | tf_op jit(solution)/shard_map/ppermute | solution.py:65
  208.6 15.0 %collective-permute-start.7 = (bf16[1,512,768]{1,2,0:T(8,128)(2,1)S(1)}, bf16[1,512,768]{1,2,0:T(8,128)(2,1)S(1)}, u32[]{:S(2)}, u32[]{:S(2)}) collective-permute-start(bf16[1,512,768]{1,2,0:T(8,128)(2,1)S(1)} %slice.256), channel_id=1, source_target_pairs={{0,2},{2,0},{4,6},{6,4},{8,10},{10,8},{12,14},{14,12},{16,18},{18,... | collective-permute-start | bytes 2359304 | tf_op jit(solution)/shard_map/ppermute | solution.py:65
  208.8 13.7 %collective-permute-start.6 = (bf16[1,512,768]{1,2,0:T(8,128)(2,1)S(1)}, bf16[1,512,768]{1,2,0:T(8,128)(2,1)S(1)}, u32[]{:S(2)}, u32[]{:S(2)}) collective-permute-start(bf16[1,512,768]{1,2,0:T(8,128)(2,1)S(1)} %slice.257), channel_id=1, source_target_pairs={{0,2},{2,0},{4,6},{6,4},{8,10},{10,8},{12,14},{14,12},{16,18},{18,... | collective-permute-start | bytes 2359304 | tf_op jit(solution)/shard_map/ppermute | solution.py:65
  220.2 69.9 %collective-permute-start.26 = (bf16[8,24,768]{2,1,0:T(8,128)(2,1)}, bf16[8,24,768]{2,1,0:T(8,128)(2,1)}, u32[]{:S(2)}, u32[]{:S(2)}) collective-permute-start(bf16[8,24,768]{2,1,0:T(8,128)(2,1)} %dynamic-slice_bitcast_fusion.12), channel_id=1, source_target_pairs={{0,1},{1,0},{2,3},{3,2},{4,5},{5,4},{6,7},{7,6},{8,9},{9,8},{10,11... | collective-permute-start | bytes 884744 | tf_op jit(solution)/shard_map/ppermute | solution.py:73
  236.5 11.7 %copy-start.38 = (f32[768]{0:T(1024)S(1)}, f32[768]{0:T(1024)}, u32[]{:S(2)}) copy-start(f32[768]{0:T(1024)} %reduce_sum.241) | copy-start | bytes 9220
  236.5 12.2 %copy-start.52 = (f32[768]{0:T(1024)S(1)}, f32[768]{0:T(1024)}, u32[]{:S(2)}) copy-start(f32[768]{0:T(1024)} %get-tuple-element.15) | copy-start | bytes 9220
  257.8 21.0 %collective-permute-start.9 = (f32[9984]{0:T(1024)}, f32[9984]{0:T(1024)S(1)}, u32[]{:S(2)}, u32[]{:S(2)}) collective-permute-start(f32[9984]{0:T(1024)} %constant_dynamic-update-slice_fusion.7), channel_id=1, source_target_pairs={{0,2},{2,0},{4,6},{6,4},{8,10},{10,8},{12,14},{14,12},{16,18},{18,... | collective-permute-start | bytes 119816 | tf_op jit(solution)/shard_map/ppermute | solution.py:65
  262.5 17.5 %copy-start.6 = (bf16[768,1152]{1,0:T(8,128)(2,1)}, bf16[768,1152]{1,0:T(8,128)(2,1)S(1)}, u32[]{:S(2)}) copy-start(bf16[768,1152]{1,0:T(8,128)(2,1)S(1)} %get-tuple-element.36) | copy-start | bytes 5308420
  262.5 17.5 %copy-start.8 = (bf16[768,1152]{1,0:T(8,128)(2,1)}, bf16[768,1152]{1,0:T(8,128)(2,1)S(1)}, u32[]{:S(2)}) copy-start(bf16[768,1152]{1,0:T(8,128)(2,1)S(1)} %get-tuple-element.35) | copy-start | bytes 5308420
  262.5 16.3 %copy-start.37 = (f32[9984]{0:T(1024)S(1)}, f32[9984]{0:T(1024)}, u32[]{:S(2)}) copy-start(f32[9984]{0:T(1024)} %constant_dynamic-update-slice_fusion.7) | copy-start | bytes 119812
  262.5 16.3 %copy-start.58 = (f32[128]{0:T(128)S(1)}, f32[128]{0:T(128)}, u32[]{:S(2)}) copy-start(f32[128]{0:T(128)} %fusion.103) | copy-start | bytes 1540
  262.5 87.1 %collective-permute-start.8 = (bf16[1,512,768]{2,1,0:T(8,128)(2,1)}, bf16[1,512,768]{2,1,0:T(8,128)(2,1)}, u32[]{:S(2)}, u32[]{:S(2)}) collective-permute-start(bf16[1,512,768]{2,1,0:T(8,128)(2,1)} %get-tuple-element.37), channel_id=1, source_target_pairs={{0,0},{1,2},{2,1},{3,3},{4,4},{5,6},{6,5},{7,7},{8,8},{9,10},{10,9... | collective-permute-start | bytes 2359304 | tf_op jit(solution)/shard_map/ppermute | solution.py:61
  270.2 81.9 %collective-permute-start.4 = (bf16[1,512,768]{2,1,0:T(8,128)(2,1)}, bf16[1,512,768]{2,1,0:T(8,128)(2,1)}, u32[]{:S(2)}, u32[]{:S(2)}) collective-permute-start(bf16[1,512,768]{2,1,0:T(8,128)(2,1)} %get-tuple-element.46), channel_id=1, source_target_pairs={{0,0},{1,2},{2,1},{3,3},{4,4},{5,6},{6,5},{7,7},{8,8},{9,10},{10,9... | collective-permute-start | bytes 2359304 | tf_op jit(solution)/shard_map/ppermute | solution.py:61
  278.9 7.1 %collective-permute-start.10 = (f32[10112]{0:T(1024)S(1)}, f32[10112]{0:T(1024)S(1)}, u32[]{:S(2)}, u32[]{:S(2)}) collective-permute-start(f32[10112]{0:T(1024)S(1)} %pad_maximum_fusion.15), channel_id=1, source_target_pairs={{0,1},{1,0},{2,3},{3,2},{4,5},{5,4},{6,7},{7,6},{8,9},{9,8},{10,11... | collective-permute-start | bytes 121352 | tf_op jit(solution)/shard_map/ppermute | solution.py:73
  286.0 66.1 %collective-permute-start.14 = (bf16[8,1,48,1152]{3,2,0,1:T(8,128)(2,1)}, bf16[8,1,48,1152]{3,2,0,1:T(8,128)(2,1)}, u32[]{:S(2)}, u32[]{:S(2)}) collective-permute-start(bf16[8,1,48,1152]{3,2,0,1:T(8,128)(2,1)} %dynamic-slice_bitcast_fusion.5), channel_id=1, source_target_pairs={{0,2},{2,0},{4,6},{6,4},{8,10},{10,8},{12,14},{14,12},{16,18},{18,... | collective-permute-start | bytes 2654216 | tf_op jit(solution)/shard_map/ppermute | solution.py:65
  290.1 4.5 collective-permute-start.11
  303.2 4.7 %collective-permute-start.12 = (f32[24320]{0:T(1024)S(1)}, f32[24320]{0:T(1024)S(1)}, u32[]{:S(2)}, u32[]{:S(2)}) collective-permute-start(f32[24320]{0:T(1024)S(1)} %pad_maximum_fusion.12), channel_id=1, source_target_pairs={{0,8},{2,10},{4,12},{6,14},{8,0},{10,2},{12,4},{14,6},{16,24},{18,... | collective-permute-start | bytes 291848 | tf_op jit(solution)/shard_map/ppermute | solution.py:65
  307.9 5.5 %collective-permute-start.27 = (bf16[4,1,24,768]{3,2,0,1:T(8,128)(2,1)}, bf16[4,1,24,768]{3,2,0,1:T(8,128)(2,1)}, u32[]{:S(2)}, u32[]{:S(2)}) collective-permute-start(bf16[4,1,24,768]{3,2,0,1:T(8,128)(2,1)} %dynamic-slice_bitcast_fusion.15), channel_id=1, source_target_pairs={{0,4},{2,6},{4,0},{6,2},{8,12},{10,14},{12,8},{14,10},{16,20},{18,... | collective-permute-start | bytes 442376 | tf_op jit(solution)/shard_map/ppermute | solution.py:65
  314.4 4.4 collective-permute-start.28
  320.1 5.8 %collective-permute-start.29 = (bf16[1,1,24,768]{3,2,0,1:T(8,128)(2,1)}, bf16[1,1,24,768]{3,2,0,1:T(8,128)(2,1)}, u32[]{:S(2)}, u32[]{:S(2)}) collective-permute-start(bf16[1,1,24,768]{3,2,0,1:T(8,128)(2,1)} %constant_dynamic-slice_fusion.2), channel_id=1, source_target_pairs={{0,16},{2,18},{4,20},{6,22},{8,24},{10,26},{12,28},{14,30},{16,0},... | collective-permute-start | bytes 110600 | tf_op jit(solution)/shard_map/ppermute | solution.py:65
  326.7 4.0 collective-permute-start.30
  330.7 8.2 %collective-permute-start.13 = (f32[43264]{0:T(1024)S(1)}, f32[43264]{0:T(1024)S(1)}, u32[]{:S(2)}, u32[]{:S(2)}) collective-permute-start(f32[43264]{0:T(1024)S(1)} %pad_maximum_fusion.10), channel_id=1, source_target_pairs={{0,16},{2,18},{4,20},{6,22},{8,24},{10,26},{12,28},{14,30},{16,0},... | collective-permute-start | bytes 519176 | tf_op jit(solution)/shard_map/ppermute | solution.py:65
  338.9 16.3 %collective-permute-start.19 = (bf16[8,1,48,1152]{3,2,0,1:T(8,128)(2,1)}, bf16[8,1,48,1152]{3,2,0,1:T(8,128)(2,1)}, u32[]{:S(2)}, u32[]{:S(2)}) collective-permute-start(bf16[8,1,48,1152]{3,2,0,1:T(8,128)(2,1)} %dynamic-slice_bitcast_fusion.4), channel_id=1, source_target_pairs={{0,2},{2,0},{4,6},{6,4},{8,10},{10,8},{12,14},{14,12},{16,18},{18,... | collective-permute-start | bytes 2654216 | tf_op jit(solution)/shard_map/ppermute | solution.py:65
  341.9 7.8 %copy-start.16 = (bf16[8,1,192,768]{3,2,0,1:T(8,128)(2,1)S(1)}, bf16[8,1,192,768]{3,2,0,1:T(8,128)(2,1)}, u32[]{:S(2)}) copy-start(bf16[8,1,192,768]{3,2,0,1:T(8,128)(2,1)} %dynamic-slice_bitcast_fusion) | copy-start | bytes 7077892
  349.7 33.0 %collective-permute-start.36 = (bf16[8,1,192,768]{3,2,0,1:T(8,128)(2,1)S(1)}, bf16[8,1,192,768]{3,2,0,1:T(8,128)(2,1)S(1)}, u32[]{:S(2)}, u32[]{:S(2)}) collective-permute-start(bf16[8,1,192,768]{3,2,0,1:T(8,128)(2,1)S(1)} %copy-done.16), channel_id=1, source_target_pairs={{0,2},{2,0},{4,6},{6,4},{8,10},{10,8},{12,14},{14,12},{16,18},{18,... | collective-permute-start | bytes 7077896 | tf_op jit(solution)/shard_map/ppermute | solution.py:65
  353.7 12.6 %collective-permute-start.15 = (bf16[4,1,48,1152]{3,2,0,1:T(8,128)(2,1)S(1)}, bf16[4,1,48,1152]{3,2,0,1:T(8,128)(2,1)S(1)}, u32[]{:S(2)}, u32[]{:S(2)}) collective-permute-start(bf16[4,1,48,1152]{3,2,0,1:T(8,128)(2,1)S(1)} %dynamic-slice_bitcast_fusion.10), channel_id=1, source_target_pairs={{0,4},{2,6},{4,0},{6,2},{8,12},{10,14},{12,8},{14,10},{16,20},{18,... | collective-permute-start | bytes 1327112 | tf_op jit(solution)/shard_map/ppermute | solution.py:65
  356.7 12.3 %collective-permute-start.20 = (bf16[8,24,1152]{2,1,0:T(8,128)(2,1)S(1)}, bf16[8,24,1152]{2,1,0:T(8,128)(2,1)S(1)}, u32[]{:S(2)}, u32[]{:S(2)}) collective-permute-start(bf16[8,24,1152]{2,1,0:T(8,128)(2,1)S(1)} %dynamic-slice_bitcast_fusion.9), channel_id=1, source_target_pairs={{0,1},{1,0},{2,3},{3,2},{4,5},{5,4},{6,7},{7,6},{8,9},{9,8},{10,11... | collective-permute-start | bytes 1327112 | tf_op jit(solution)/shard_map/ppermute | solution.py:73
  366.5 7.1 %collective-permute-start.16 = (bf16[2,1,48,1152]{3,2,0,1:T(8,128)(2,1)S(1)}, bf16[2,1,48,1152]{3,2,0,1:T(8,128)(2,1)S(1)}, u32[]{:S(2)}, u32[]{:S(2)}) collective-permute-start(bf16[2,1,48,1152]{3,2,0,1:T(8,128)(2,1)S(1)} %dynamic-slice_bitcast_fusion.14), channel_id=1, source_target_pairs={{0,8},{2,10},{4,12},{6,14},{8,0},{10,2},{12,4},{14,6},{16,24},{18,... | collective-permute-start | bytes 663560 | tf_op jit(solution)/shard_map/ppermute | solution.py:65
  369.2 6.8 %collective-permute-start.21 = (bf16[4,1,24,1152]{3,2,0,1:T(8,128)(2,1)S(1)}, bf16[4,1,24,1152]{3,2,0,1:T(8,128)(2,1)S(1)}, u32[]{:S(2)}, u32[]{:S(2)}) collective-permute-start(bf16[4,1,24,1152]{3,2,0,1:T(8,128)(2,1)S(1)} %dynamic-slice_bitcast_fusion.13), channel_id=1, source_target_pairs={{0,4},{2,6},{4,0},{6,2},{8,12},{10,14},{12,8},{14,10},{16,20},{18,... | collective-permute-start | bytes 663560 | tf_op jit(solution)/shard_map/ppermute | solution.py:65
  373.7 16.1 %collective-permute-start.17 = (bf16[1,1,48,1152]{3,2,0,1:T(8,128)(2,1)S(1)}, bf16[1,1,48,1152]{3,2,0,1:T(8,128)(2,1)S(1)}, u32[]{:S(2)}, u32[]{:S(2)}) collective-permute-start(bf16[1,1,48,1152]{3,2,0,1:T(8,128)(2,1)S(1)} %constant_dynamic-slice_fusion.4), channel_id=1, source_target_pairs={{0,16},{2,18},{4,20},{6,22},{8,24},{10,26},{12,28},{14,30},{16,0},... | collective-permute-start | bytes 331784 | tf_op jit(solution)/shard_map/ppermute | solution.py:65
  376.1 6.6 %slice-start = ((s8[4718592]{0:T(1024)(128)(4,1)}), s8[4194304]{0:T(1024)(128)(4,1)S(1)}, s32[]{:S(2)}) async-start(s8[4718592]{0:T(1024)(128)(4,1)} %bitcast.292), calls=%async_computation | async-start | bytes 8388608
  376.1 6.5 %slice-start.1 = ((s8[4718592]{0:T(1024)(128)(4,1)}), s8[524288]{0:T(1024)(128)(4,1)S(1)}, s32[]{:S(2)}) async-start(s8[4718592]{0:T(1024)(128)(4,1)} %bitcast.292), calls=%async_computation.1 | async-start | bytes 1048576
  376.1 7.1 %collective-permute-start.22 = (bf16[2,1,24,1152]{3,2,1,0:T(8,128)(2,1)S(1)}, bf16[2,1,24,1152]{3,2,1,0:T(8,128)(2,1)S(1)}, u32[]{:S(2)}, u32[]{:S(2)}) collective-permute-start(bf16[2,1,24,1152]{3,2,1,0:T(8,128)(2,1)S(1)} %dynamic-slice_bitcast_fusion.16), channel_id=1, source_target_pairs={{0,8},{2,10},{4,12},{6,14},{8,0},{10,2},{12,4},{14,6},{16,24},{18,... | collective-permute-start | bytes 331784 | tf_op jit(solution)/shard_map/ppermute | solution.py:65
  381.0 33.6 %collective-permute-start.32 = (bf16[4,1,48,3072]{3,2,0,1:T(8,128)(2,1)S(1)}, bf16[4,1,48,3072]{3,2,0,1:T(8,128)(2,1)S(1)}, u32[]{:S(2)}, u32[]{:S(2)}) collective-permute-start(bf16[4,1,48,3072]{3,2,0,1:T(8,128)(2,1)S(1)} %dynamic-slice_bitcast_fusion.3), channel_id=1, source_target_pairs={{0,4},{2,6},{4,0},{6,2},{8,12},{10,14},{12,8},{14,10},{16,20},{18,... | collective-permute-start | bytes 3538952 | tf_op jit(solution)/shard_map/ppermute | solution.py:65
  383.3 5.6 %collective-permute-start.23 = (bf16[1,1,24,1152]{3,2,1,0:T(8,128)(2,1)S(1)}, bf16[1,1,24,1152]{3,2,1,0:T(8,128)(2,1)S(1)}, u32[]{:S(2)}, u32[]{:S(2)}) collective-permute-start(bf16[1,1,24,1152]{3,2,1,0:T(8,128)(2,1)S(1)} %constant_dynamic-slice_fusion.3), channel_id=1, source_target_pairs={{0,16},{2,18},{4,20},{6,22},{8,24},{10,26},{12,28},{14,30},{16,0},... | collective-permute-start | bytes 165896 | tf_op jit(solution)/shard_map/ppermute | solution.py:65
  384.7 28.1 %collective-permute-start.37 = (bf16[8,96,768]{2,1,0:T(8,128)(2,1)S(1)}, bf16[8,96,768]{2,1,0:T(8,128)(2,1)S(1)}, u32[]{:S(2)}, u32[]{:S(2)}) collective-permute-start(bf16[8,96,768]{2,1,0:T(8,128)(2,1)S(1)} %dynamic-slice_bitcast_fusion.2), channel_id=1, source_target_pairs={{0,1},{1,0},{2,3},{3,2},{4,5},{5,4},{6,7},{7,6},{8,9},{9,8},{10,11... | collective-permute-start | bytes 3538952 | tf_op jit(solution)/shard_map/ppermute | solution.py:73
  388.9 23.9 %collective-permute-start.24 = (bf16[24,1152]{1,0:T(8,128)(2,1)S(1)}, bf16[24,1152]{1,0:T(8,128)(2,1)S(1)}, u32[]{:S(2)}, u32[]{:S(2)}) collective-permute-start(bf16[24,1152]{1,0:T(8,128)(2,1)S(1)} %fusion.75), channel_id=1, source_target_pairs={{0,1},{1,0},{2,3},{3,2},{4,5},{5,4},{6,7},{7,6},{8,9},{9,8},{10,11... | collective-permute-start | bytes 165896 | tf_op jit(solution)/shard_map/ppermute | solution.py:73
  389.8 25.8 %collective-permute-start.18 = (bf16[48,1152]{1,0:T(8,128)(2,1)S(1)}, bf16[48,1152]{1,0:T(8,128)(2,1)S(1)}, u32[]{:S(2)}, u32[]{:S(2)}) collective-permute-start(bf16[48,1152]{1,0:T(8,128)(2,1)S(1)} %fusion.74), channel_id=1, source_target_pairs={{0,1},{1,0},{2,3},{3,2},{4,5},{5,4},{6,7},{7,6},{8,9},{9,8},{10,11... | collective-permute-start | bytes 331784 | tf_op jit(solution)/shard_map/ppermute | solution.py:73
  413.2 11.0 %collective-permute-start.38 = (bf16[4,1,96,768]{3,2,0,1:T(8,128)(2,1)S(1)}, bf16[4,1,96,768]{3,2,0,1:T(8,128)(2,1)S(1)}, u32[]{:S(2)}, u32[]{:S(2)}) collective-permute-start(bf16[4,1,96,768]{3,2,0,1:T(8,128)(2,1)S(1)} %dynamic-slice_bitcast_fusion.6), channel_id=1, source_target_pairs={{0,4},{2,6},{4,0},{6,2},{8,12},{10,14},{12,8},{14,10},{16,20},{18,... | collective-permute-start | bytes 1769480 | tf_op jit(solution)/shard_map/ppermute | solution.py:65
  415.1 16.9 %collective-permute-start.33 = (bf16[2,1,48,3072]{3,2,0,1:T(8,128)(2,1)S(1)}, bf16[2,1,48,3072]{3,2,0,1:T(8,128)(2,1)S(1)}, u32[]{:S(2)}, u32[]{:S(2)}) collective-permute-start(bf16[2,1,48,3072]{3,2,0,1:T(8,128)(2,1)S(1)} %dynamic-slice_bitcast_fusion.7), channel_id=1, source_target_pairs={{0,8},{2,10},{4,12},{6,14},{8,0},{10,2},{12,4},{14,6},{16,24},{18,... | collective-permute-start | bytes 1769480 | tf_op jit(solution)/shard_map/ppermute | solution.py:65
  424.4 10.7 %collective-permute-start.39 = (bf16[2,1,96,768]{3,2,0,1:T(8,128)(2,1)S(1)}, bf16[2,1,96,768]{3,2,0,1:T(8,128)(2,1)S(1)}, u32[]{:S(2)}, u32[]{:S(2)}) collective-permute-start(bf16[2,1,96,768]{3,2,0,1:T(8,128)(2,1)S(1)} %dynamic-slice_bitcast_fusion.11), channel_id=1, source_target_pairs={{0,8},{2,10},{4,12},{6,14},{8,0},{10,2},{12,4},{14,6},{16,24},{18,... | collective-permute-start | bytes 884744 | tf_op jit(solution)/shard_map/ppermute | solution.py:65
  432.2 16.8 %collective-permute-start.34 = (bf16[1,1,48,3072]{3,2,0,1:T(8,128)(2,1)S(1)}, bf16[1,1,48,3072]{3,2,0,1:T(8,128)(2,1)S(1)}, u32[]{:S(2)}, u32[]{:S(2)}) collective-permute-start(bf16[1,1,48,3072]{3,2,0,1:T(8,128)(2,1)S(1)} %constant_dynamic-slice_fusion.1), channel_id=1, source_target_pairs={{0,16},{2,18},{4,20},{6,22},{8,24},{10,26},{12,28},{14,30},{16,0},... | collective-permute-start | bytes 884744 | tf_op jit(solution)/shard_map/ppermute | solution.py:65
  435.2 12.8 %collective-permute-start.40 = (bf16[1,1,96,768]{3,2,0,1:T(8,128)(2,1)S(1)}, bf16[1,1,96,768]{3,2,0,1:T(8,128)(2,1)S(1)}, u32[]{:S(2)}, u32[]{:S(2)}) collective-permute-start(bf16[1,1,96,768]{3,2,0,1:T(8,128)(2,1)S(1)} %constant_dynamic-slice_fusion), channel_id=1, source_target_pairs={{0,16},{2,18},{4,20},{6,22},{8,24},{10,26},{12,28},{14,30},{16,0},... | collective-permute-start | bytes 442376 | tf_op jit(solution)/shard_map/ppermute | solution.py:65
  448.1 5.5 %collective-permute-start.41 = (bf16[96,768]{1,0:T(8,128)(2,1)S(1)}, bf16[96,768]{1,0:T(8,128)(2,1)S(1)}, u32[]{:S(2)}, u32[]{:S(2)}) collective-permute-start(bf16[96,768]{1,0:T(8,128)(2,1)S(1)} %fusion.72), channel_id=1, source_target_pairs={{0,1},{1,0},{2,3},{3,2},{4,5},{5,4},{6,7},{7,6},{8,9},{9,8},{10,11... | collective-permute-start | bytes 442376 | tf_op jit(solution)/shard_map/ppermute | solution.py:73
  449.0 7.8 %collective-permute-start.35 = (bf16[48,3072]{1,0:T(8,128)(2,1)S(1)}, bf16[48,3072]{1,0:T(8,128)(2,1)S(1)}, u32[]{:S(2)}, u32[]{:S(2)}) collective-permute-start(bf16[48,3072]{1,0:T(8,128)(2,1)S(1)} %fusion.69), channel_id=1, source_target_pairs={{0,1},{1,0},{2,3},{3,2},{4,5},{5,4},{6,7},{7,6},{8,9},{9,8},{10,11... | collective-permute-start | bytes 884744 | tf_op jit(solution)/shard_map/ppermute | solution.py:73
  (44 other events, 122.3 us)

commit v2 on v1

v2 whole, which is shorter than its diff:
```python
import jax
import jax.numpy as jnp
from jax import lax
from jax.experimental import pallas as pl
from jax.experimental.pallas import tpu as pltpu
from jax.sharding import PartitionSpec as P

HD = 64


highest = lax.Precision.HIGHEST


def tables(positions):
    half_dim = HD // 2
    frequency = jnp.exp(
        -jnp.log(10000.0) * (2.0 * jnp.arange(half_dim, dtype=jnp.float32) / HD)
    )
    angles = positions.astype(jnp.float32)[:, None] * frequency[None, :]
    cosine, sine = jnp.cos(angles), jnp.sin(angles)
    return (
        jnp.concatenate([cosine] * 4, axis=1),
        jnp.concatenate([-sine, sine, -sine, sine], axis=1),
    )


def full(shape):
    return pl.BlockSpec(shape, lambda step: (0,) * len(shape))


def columns(rows, width, first=0):
    return pl.BlockSpec((rows, width), lambda step: (0, step + first))


def shaped(shape, kind):
    return jax.ShapeDtypeStruct(shape, kind)


def kernel_call(body, steps, in_specs, out_specs, out_shape, scratch, flops, moved):
    return pl.pallas_call(
        body,
        grid=(steps,),
        in_specs=in_specs,
        out_specs=out_specs,
        out_shape=out_shape,
        scratch_shapes=scratch,
        compiler_params=pltpu.CompilerParams(
            dimension_semantics=("arbitrary",), vmem_limit_bytes=56 * 1024 * 1024
        ),
        cost_estimate=pl.CostEstimate(flops=flops, bytes_accessed=moved, transcendentals=0),
    )


def dot(left, right, left_axis=1, right_axis=0):
    return lax.dot_general(
        left,
        right,
        (((left_axis,), (right_axis,)), ((), ())),
        preferred_element_type=jnp.float32,
    )


def normalized(inputs):
    center = inputs - jnp.mean(inputs, axis=-1, keepdims=True)
    inverse = lax.rsqrt(jnp.mean(center * center, axis=-1, keepdims=True) + 1e-05)
    return center * inverse, inverse


def norm_back(back, hat, inverse, factor):
    scaled = back * factor
    return inverse * (
        scaled
        - jnp.mean(scaled, axis=-1, keepdims=True)
        - hat * jnp.mean(scaled * hat, axis=-1, keepdims=True)
    )


def column_sum(values):
    return jnp.sum(values, axis=0, keepdims=True)


SHIFT1, SCALE1, GATE1, SHIFT2, SCALE2, GATE2, GAIN1, GAIN2 = range(8)


def row(ref, index):
    return ref[index : index + 1, :]


def rotate_lanes(values, cosine, sine):
    lane = lax.broadcasted_iota(jnp.int32, cosine.shape, 1)
    lower = (lane % HD) < HD // 2
    parts = []
    for start in range(0, values.shape[1], 128):
        part = values[:, start : start + 128]
        other = jnp.where(lower, pltpu.roll(part, 128 - HD // 2, 1), pltpu.roll(part, HD // 2, 1))
        parts.append(part * cosine + other * sine)
    return jnp.concatenate(parts, axis=1)


COLUMNS = 384


def key_value_body(tokens, mods, weight, cosine, sine, normed, out):
    step = pl.program_id(0)
    turned_steps = pl.num_programs(0) // 2

    @pl.when(step == 0)
    def _():
        hat, _ = normalized(tokens[...].astype(jnp.float32))
        value = hat * row(mods, GAIN1) * (1.0 + row(mods, SCALE1)) + row(mods, SHIFT1)
        normed[...] = value.astype(jnp.bfloat16)

    @pl.when(step < turned_steps)
    def _():
        value = dot(normed[...], weight[...])
        out[...] = rotate_lanes(value, cosine[...], sine[...]).astype(jnp.bfloat16)

    @pl.when(step >= turned_steps)
    def _():
        out[...] = dot(normed[...], weight[...]).astype(jnp.bfloat16)


def project_key_value(tokens, mods, weight, cosine, sine):
    rows, width = tokens.shape
    first = width // COLUMNS
    return kernel_call(
        key_value_body,
        2 * first,
        [
            full((rows, width)),
            full((8, width)),
            columns(width, COLUMNS, first),
            full((rows, 128)),
            full((rows, 128)),
        ],
        [full((rows, width)), columns(rows, COLUMNS)],
        [shaped((rows, width), jnp.bfloat16), shaped((rows, 2 * width), jnp.bfloat16)],
        [],
        4 * rows * width * width,
        8 * width * width,
    )(tokens, mods, weight, cosine, sine)


def query_body(normed, weight, cosine, sine, out):
    value = dot(normed[...], weight[...])
    out[...] = rotate_lanes(value, cosine[...], sine[...]).astype(jnp.bfloat16)


def project_query(normed, weight, cosine, sine):
    rows, width = normed.shape
    return kernel_call(
        query_body,
        width // COLUMNS,
        [full((rows, width)), columns(width, COLUMNS), full((rows, 128)), full((rows, 128))],
        columns(rows, COLUMNS),
        shaped((rows, width), jnp.bfloat16),
        [],
        2 * rows * width * width,
        4 * width * width,
    )(normed, weight, cosine, sine)


def head_mask(shape, head, value):
    lane = lax.broadcasted_iota(jnp.int32, shape, 1)
    return jnp.where(lane // HD == head, value, 0.0).astype(jnp.bfloat16)


def attend_body(query, keys1, values1, keys2, values2, out, log_total):
    rows = query.shape[0]
    turned1 = values1[...].T
    turned2 = values2[...].T
    parts = []
    for head in range(2):
        own = query[...] * head_mask((rows, 128), head, HD ** (-0.5))
        scores1 = dot(keys1[...], own, 1, 1)
        scores2 = dot(keys2[...], own, 1, 1)
        top = jnp.maximum(
            jnp.max(scores1, axis=0, keepdims=True), jnp.max(scores2, axis=0, keepdims=True)
        )
        exps1 = jnp.exp(scores1 - top)
        exps2 = jnp.exp(scores2 - top)
        total = column_sum(exps1) + column_sum(exps2)
        lanes = slice(head * HD, (head + 1) * HD)
        mixed = dot(turned1[lanes], exps1.astype(jnp.bfloat16)) + dot(
            turned2[lanes], exps2.astype(jnp.bfloat16)
        )
        parts.append(mixed / total)
        log_total[0, head : head + 1, :] = top + jnp.log(total)
    out[...] = jnp.concatenate(parts, axis=0).T.astype(jnp.bfloat16)


def attend(query, own, peer):
    rows, width = query.shape
    pairs = width // 128
    return kernel_call(
        attend_body,
        pairs,
        [
            columns(rows, 128),
            columns(rows, 128),
            columns(rows, 128, pairs),
            columns(rows, 128),
            columns(rows, 128, pairs),
        ],
        [columns(rows, 128), pl.BlockSpec((1, 2, rows), lambda step: (step, 0, 0))],
        [shaped((rows, width), jnp.bfloat16), shaped((pairs, 2, rows), jnp.float32)],
        [],
        16 * rows * rows * width,
        8 * rows * width,
    )(query, own, own, peer, peer)


def attend_back_body(query, keys, values, grad, attended, log_total, *refs):
    if len(refs) == 4:
        before, d_query, d_keys, d_values = refs
    else:
        before, (d_query, d_keys, d_values) = None, refs
    rows = query.shape[0]
    keys_turned = keys[...].T
    product = (grad[...].astype(jnp.float32) * attended[...].astype(jnp.float32)).T
    parts = []
    keys_sum = values_sum = None
    for head in range(2):
        lanes = slice(head * HD, (head + 1) * HD)
        own = query[...] * head_mask((rows, 128), head, HD ** (-0.5))
        own_grad = grad[...] * head_mask((rows, 128), head, 1.0)
        delta = column_sum(product[lanes])
        scores = dot(keys[...], own, 1, 1)
        probs = jnp.exp(scores - log_total[0, head : head + 1, :])
        d_probs = dot(values[...], own_grad, 1, 1)
        d_scores = (probs * (d_probs - delta)).astype(jnp.bfloat16)
        values_part = dot(probs.astype(jnp.bfloat16), own_grad)
        keys_part = dot(d_scores, own)
        values_sum = values_part if values_sum is None else values_sum + values_part
        keys_sum = keys_part if keys_sum is None else keys_sum + keys_part
        parts.append(dot(keys_turned[lanes], d_scores))
    turned = jnp.concatenate(parts, axis=0).T * HD ** (-0.5)
    d_query[...] = turned if before is None else turned + before[...]
    d_keys[...] = keys_sum.astype(d_keys.dtype)
    d_values[...] = values_sum.astype(d_values.dtype)


def attend_back(query, pair, grad, attended, log_total, before, kind):
    rows, width = query.shape
    pairs = width // 128
    block = columns(rows, 128)
    extra = [] if before is None else [before]
    return kernel_call(
        attend_back_body,
        pairs,
        [
            block,
            block,
            columns(rows, 128, pairs),
            block,
            block,
            pl.BlockSpec((1, 2, rows), lambda step: (step, 0, 0)),
        ]
        + [block] * len(extra),
        [block, block, block],
        [
            shaped((rows, width), jnp.float32),
            shaped((rows, width), kind),
            shaped((rows, width), kind),
        ],
        [],
        20 * rows * rows * width,
        20 * rows * width,
    )(query, pair, pair, grad, attended, log_total, *extra)


def up_body(
    attended, tokens, cotangent, mods, out_weight, up_weight, bias,
    branch, middle, normed, d_ffn, activated, slope, down_grad,
):
    @pl.when(pl.program_id(0) == 0)
    def _():
        mixed = dot(attended[...], out_weight[...])
        branch[...] = mixed
        value = tokens[...].astype(jnp.float32) + row(mods, GATE1) * mixed
        middle[...] = value
        hat, _ = normalized(value)
        value = hat * row(mods, GAIN2) * (1.0 + row(mods, SCALE2)) + row(mods, SHIFT2)
        normed[...] = value.astype(jnp.bfloat16)
        d_ffn[...] = (row(mods, GATE2) * cotangent[...].astype(jnp.float32)).astype(jnp.bfloat16)

    pre = dot(normed[...], up_weight[...]) + bias[...]
    root = 0.7978845608028654
    square = pre * pre
    bent = jnp.tanh(root * pre * (1.0 + 0.044715 * square))
    half = 0.5 + 0.5 * bent
    slope[...] = (
        half + 0.5 * root * pre * (1.0 - bent * bent) * (1.0 + 0.134145 * square)
    ).astype(jnp.bfloat16)
    low = (pre * half).astype(jnp.bfloat16)
    activated[...] = low
    down_grad[...] = dot(low, d_ffn[...], 0, 0).astype(jnp.bfloat16)


def up_layer(attended, tokens, cotangent, mods, out_weight, up_weight, bias):
    rows, width = tokens.shape
    hidden = up_weight.shape[1]
    block = full((rows, width))
    tile = 512
    return kernel_call(
        up_body,
        hidden // tile,
        [
            block,
            block,
            block,
            full((8, width)),
            full((width, width)),
            columns(width, tile),
            columns(1, tile),
        ],
        [
            block,
            block,
            block,
            block,
            columns(rows, tile),
            columns(rows, tile),
            pl.BlockSpec((tile, width), lambda step: (step, 0)),
        ],
        [
            shaped((rows, width), jnp.float32),
            shaped((rows, width), jnp.float32),
            shaped((rows, width), jnp.bfloat16),
            shaped((rows, width), jnp.bfloat16),
            shaped((rows, hidden), jnp.bfloat16),
            shaped((rows, hidden), jnp.bfloat16),
            shaped((hidden, width), jnp.bfloat16),
        ],
        [],
        4 * rows * width * hidden + 2 * rows * width * width,
        8 * rows * hidden + 4 * hidden * width,
    )(attended, tokens, cotangent, mods, out_weight, up_weight, bias)


def up_back_body(d_ffn, normed, down_weight, slope, d_pre, up_grad, bias_grad):
    value = dot(d_ffn[...], down_weight[...], 1, 1) * slope[...].astype(jnp.float32)
    low = value.astype(jnp.bfloat16)
    d_pre[...] = low
    bias_grad[...] = column_sum(value)
    up_grad[...] = dot(normed[...], low, 0, 0).astype(jnp.bfloat16)


def up_back(d_ffn, normed, down_weight, slope):
    rows, width = normed.shape
    hidden = down_weight.shape[0]
    tile = 512
    return kernel_call(
        up_back_body,
        hidden // tile,
        [
            full((rows, width)),
            full((rows, width)),
            pl.BlockSpec((tile, width), lambda step: (step, 0)),
            columns(rows, tile),
        ],
        [columns(rows, tile), columns(width, tile), columns(1, tile)],
        [
            shaped((rows, hidden), jnp.bfloat16),
            shaped((width, hidden), jnp.bfloat16),
            shaped((1, hidden), jnp.float32),
        ],
        [],
        4 * rows * width * hidden,
        8 * rows * hidden + 4 * hidden * width,
    )(d_ffn, normed, down_weight, slope)


def down_body(
    activated, d_pre, down_weight, up_weight, cotangent, d_ffn, middle, branch, attended,
    mods, out_weight, bias,
    mixed, d_middle, d_attended, out_grad, sums, forward, backward,
):
    step = pl.program_id(0)

    @pl.when(step == 0)
    def _():
        forward[...] = jnp.zeros_like(forward)
        backward[...] = jnp.zeros_like(backward)

    forward[...] += dot(activated[...], down_weight[...])
    backward[...] += dot(d_pre[...], up_weight[...], 1, 1)

    @pl.when(step == pl.num_programs(0) - 1)
    def _():
        ffn = forward[...] + bias[...]
        value = middle[...]
        grad = cotangent[...].astype(jnp.float32)
        mixed[...] = (value + row(mods, GATE2) * ffn).astype(jnp.bfloat16)
        back = backward[...]
        hat, inverse = normalized(value)
        d_value = grad + norm_back(
            back, hat, inverse, row(mods, GAIN2) * (1.0 + row(mods, SCALE2))
        )
        d_middle[...] = d_value
        d_branch = (row(mods, GATE1) * d_value).astype(jnp.bfloat16)
        out_grad[...] = dot(attended[...], d_branch, 0, 0).astype(jnp.bfloat16)
        d_attended[...] = dot(d_branch, out_weight[...], 1, 1).astype(jnp.bfloat16)
        sums[0:1, :] = column_sum(back)
        sums[1:2, :] = column_sum(back * hat)
        sums[2:3, :] = column_sum(d_value * branch[...])
        sums[3:4, :] = column_sum(grad * ffn)
        sums[4:5, :] = column_sum(d_ffn[...].astype(jnp.float32))
        sums[5:8, :] = jnp.zeros_like(sums[5:8, :])


def down_layer(
    activated, d_pre, down_weight, up_weight, cotangent, d_ffn, middle, branch, attended,
    mods, out_weight, bias,
):
    rows, width = middle.shape
    hidden = down_weight.shape[0]
    tile = 512
    block = full((rows, width))
    return kernel_call(
        down_body,
        hidden // tile,
        [
            columns(rows, tile),
            columns(rows, tile),
            pl.BlockSpec((tile, width), lambda step: (step, 0)),
            columns(width, tile),
            block,
            block,
            block,
            block,
            block,
            full((8, width)),
            full((width, width)),
            full((1, width)),
        ],
        [block, block, block, full((width, width)), full((8, width))],
        [
            shaped((rows, width), jnp.bfloat16),
            shaped((rows, width), jnp.float32),
            shaped((rows, width), jnp.bfloat16),
            shaped((width, width), jnp.bfloat16),
            shaped((8, width), jnp.float32),
        ],
        [pltpu.VMEM((rows, width), jnp.float32), pltpu.VMEM((rows, width), jnp.float32)],
        4 * rows * width * hidden + 4 * rows * width * width,
        4 * rows * hidden + 4 * hidden * width,
    )(
        activated, d_pre, down_weight, up_weight, cotangent, d_ffn, middle, branch, attended,
        mods, out_weight, bias,
    )


def projected_back_body(
    d_query, d_keys, d_values, peer_keys, peer_values, normed, cosine, sine, d_projected, grad
):
    step = pl.program_id(0)
    per_part = pl.num_programs(0) // 3

    def finish(low):
        d_projected[...] = low
        grad[...] = dot(normed[...], low, 0, 0).astype(jnp.bfloat16)

    @pl.when(step < per_part)
    def _():
        finish(rotate_lanes(d_query[...], cosine[...], -sine[...]).astype(jnp.bfloat16))

    @pl.when((step >= per_part) & (step < 2 * per_part))
    def _():
        value = d_keys[...] + peer_keys[...].astype(jnp.float32)
        finish(rotate_lanes(value, cosine[...], -sine[...]).astype(jnp.bfloat16))

    @pl.when(step >= 2 * per_part)
    def _():
        value = d_values[...] + peer_values[...].astype(jnp.float32)
        finish(value.astype(jnp.bfloat16))


def projected_back(d_query, d_keys, d_values, peer_keys, peer_values, normed, cosine, sine):
    rows, width = normed.shape
    per_part = width // COLUMNS

    def part(index):
        return pl.BlockSpec(
            (rows, COLUMNS),
            lambda step: (0, jnp.clip(step - index * per_part, 0, per_part - 1)),
        )

    return kernel_call(
        projected_back_body,
        3 * per_part,
        [
            part(0),
            part(1),
            part(2),
            part(1),
            part(2),
            full((rows, width)),
            full((rows, 128)),
            full((rows, 128)),
        ],
        [columns(rows, COLUMNS), columns(width, COLUMNS)],
        [shaped((rows, 3 * width), jnp.bfloat16), shaped((width, 3 * width), jnp.bfloat16)],
        [],
        6 * rows * width * width,
        22 * rows * width,
    )(d_query, d_keys, d_values, peer_keys, peer_values, normed, cosine, sine)


def tokens_back_body(d_projected, weight, tokens, d_middle, mods, out, sums, total):
    step = pl.program_id(0)

    @pl.when(step == 0)
    def _():
        total[...] = jnp.zeros_like(total)

    total[...] += dot(d_projected[...], weight[...], 1, 1)

    @pl.when(step == pl.num_programs(0) - 1)
    def _():
        back = total[...]
        hat, inverse = normalized(tokens[...].astype(jnp.float32))
        factor = row(mods, GAIN1) * (1.0 + row(mods, SCALE1))
        out[...] = (d_middle[...] + norm_back(back, hat, inverse, factor)).astype(jnp.bfloat16)
        sums[0:1, :] = column_sum(back)
        sums[1:2, :] = column_sum(back * hat)
        sums[2:8, :] = jnp.zeros_like(sums[2:8, :])


def tokens_back(d_projected, weight, tokens, d_middle, mods):
    rows, width = tokens.shape
    block = full((rows, width))
    return kernel_call(
        tokens_back_body,
        3 * width // COLUMNS,
        [columns(rows, COLUMNS), columns(width, COLUMNS), block, block, full((8, width))],
        [block, full((8, width))],
        [shaped((rows, width), jnp.bfloat16), shaped((8, width), jnp.float32)],
        [pltpu.VMEM((rows, width), jnp.float32)],
        6 * rows * width * width,
        6 * width * width + 10 * rows * width,
    )(d_projected, weight, tokens, d_middle, mods)


def swap_halves(block):
    count = lax.axis_size("dp") * lax.axis_size("seq")
    target = {1: 2, 2: 1}
    perm = [(i, i - i % 4 + target.get(i % 4, i % 4)) for i in range(count)]
    return lax.ppermute(block, ("dp", "seq"), perm)


def swap_bit(block, bit):
    return lax.ppermute(block, "dp", [(i, i ^ bit) for i in range(lax.axis_size("dp"))])


def swap_cores(block):
    return swap_bit(block, 1)


def swap_seq(block):
    return lax.ppermute(block, "seq", [(0, 1), (1, 0)])


def dp_bits():
    bits, bit = [], 1
    while bit < lax.axis_size("dp"):
        bits.append(bit)
        bit *= 2
    return bits


def pick(block, axis, index):
    return lax.dynamic_index_in_dim(block, index, axis, keepdims=False)


def scatter_sum(matrix, seq_first):
    dp_size = lax.axis_size("dp")
    dp_rank = lax.axis_index("dp")
    seq_rank = lax.axis_index("seq")
    rows, columns = matrix.shape
    own = rows // dp_size
    low = jnp.bfloat16
    block = matrix.reshape(dp_size, own, columns)

    def by_bit(block, bit, done):
        mine = (dp_rank // bit) % 2
        count, rest, width = block.shape
        inner = 1
        low_bit = 1
        while low_bit < bit:
            if low_bit not in done:
                inner *= 2
            low_bit *= 2
        split = block.reshape(count // (2 * inner), 2, inner, rest, width)
        got = swap_bit(pick(split, 1, 1 - mine), bit)
        kept = pick(split, 1, mine)
        total = kept.astype(jnp.float32) + got.astype(jnp.float32)
        return total.astype(low).reshape(count // 2, rest, width)

    block = by_bit(block, 1, [])
    done = [1]
    if seq_first:
        count, rest, width = block.shape
        split = block.reshape(count, 2, rest // 2, width)
        got = swap_seq(pick(split, 1, 1 - seq_rank))
        total = pick(split, 1, seq_rank).astype(jnp.float32) + got.astype(jnp.float32)
        block = total.astype(low)
    for bit in dp_bits()[1:]:
        block = by_bit(block, bit, done)
        done.append(bit)
    block = block[0]
    got = swap_seq(block)
    if seq_first:
        first = jnp.where(seq_rank == 0, block, got)
        second = jnp.where(seq_rank == 0, got, block)
        return jnp.concatenate([first, second], axis=0).astype(jnp.float32)
    return block.astype(jnp.float32) + got.astype(jnp.float32)


def share_small(per_sequence, cond, summed):
    dp_rank = lax.axis_index("dp")
    seq_rank = lax.axis_index("seq")
    sizes = [part.shape[0] for part in summed]
    totals = jnp.concatenate(summed)
    joined = jnp.concatenate([per_sequence[0], totals])
    joined = joined + swap_cores(joined)
    width = per_sequence.shape[1]
    gathered = jnp.concatenate([joined[:width], cond[0]])[None]
    totals = joined[width:]

    def double(gathered, totals, mine, move):
        count = gathered.shape[0]
        sent = jnp.concatenate([gathered.reshape(-1), totals])
        got = move(sent)
        theirs = got[: gathered.size].reshape(gathered.shape)
        first = jnp.where(mine == 0, gathered, theirs)
        second = jnp.where(mine == 0, theirs, gathered)
        return jnp.concatenate([first, second], axis=0), totals + got[gathered.size :]

    gathered, totals = double(gathered, totals, seq_rank, swap_seq)
    for bit in dp_bits()[1:]:
        gathered, totals = double(
            gathered, totals, (dp_rank // bit) % 2, lambda sent, bit=bit: swap_bit(sent, bit)
        )
    parts, start = [], 0
    for size in sizes:
        parts.append(totals[start : start + size])
        start += size
    return gathered[:, :width], gathered[:, width:], parts


def per_device(
    tokens,
    cotangent,
    time_index,
    step_table,
    first_gain,
    attn_qkv,
    attn_out,
    second_gain,
    mlp_up,
    up_bias,
    mlp_down,
    down_bias,
    ada_weight,
    ada_bias,
):
    rows, width = tokens.shape[1:]
    dp_rank = lax.axis_index("dp")
    core = dp_rank % 2
    own_cond, silu_back = jax.vjp(
        jax.nn.silu, lax.dynamic_slice_in_dim(step_table, time_index[0], 1, axis=0)
    )
    tokens = swap_halves(tokens[0])
    time_index = swap_halves(time_index)
    cotangent = swap_halves(cotangent[0])
    cond = jax.nn.silu(lax.dynamic_slice_in_dim(step_table, time_index[0], 1, axis=0))
    ada_float = ada_weight.astype(jnp.float32)
    modulation = jnp.dot(cond, ada_float, precision=highest) + ada_bias.astype(jnp.float32)
    gain1 = first_gain.astype(jnp.float32)
    gain2 = second_gain.astype(jnp.float32)
    mods = jnp.concatenate([modulation.reshape(6, width), gain1[None], gain2[None]])
    positions = core * rows + jnp.arange(rows, dtype=jnp.int32)
    cosine, sine = tables(positions)

    normed1, own_pair = project_key_value(tokens, mods, attn_qkv, cosine, sine)
    peer_pair = swap_cores(own_pair)
    query = project_query(normed1, attn_qkv, cosine, sine)
    attended, log_total = attend(query, own_pair, peer_pair)
    branch, middle, normed2, d_ffn, activated, slope, mlp_down_grad = up_layer(
        attended, tokens, cotangent, mods, attn_out, mlp_up, up_bias.astype(jnp.float32)[None]
    )
    d_pre, mlp_up_grad, up_bias_grad = up_back(d_ffn, normed2, mlp_down, slope)
    mixed, d_middle, d_attended, attn_out_grad, sums2 = down_layer(
        activated, d_pre, mlp_down, mlp_up, cotangent, d_ffn, middle, branch, attended,
        mods, attn_out, down_bias.astype(jnp.float32)[None],
    )
    d_query, away_keys, away_values = attend_back(
        query, peer_pair, d_attended, attended, log_total, None, jnp.bfloat16
    )
    peer_keys, peer_values = swap_cores(away_keys), swap_cores(away_values)
    d_query, d_keys, d_values = attend_back(
        query, own_pair, d_attended, attended, log_total, d_query, jnp.float32
    )
    d_projected, attn_qkv_grad = projected_back(
        d_query, d_keys, d_values, peer_keys, peer_values, normed1, cosine, sine
    )
    tokens_grad, sums1 = tokens_back(d_projected, attn_qkv, tokens, d_middle, mods)

    d_modulation = jnp.concatenate(
        [sums1[0], sums1[1] * gain1, sums2[2], sums2[0], sums2[1] * gain2, sums2[3]]
    )[None]
    first_gain_grad = sums1[1] * (1.0 + mods[SCALE1])
    second_gain_grad = sums2[1] * (1.0 + mods[SCALE2])
    d_mod_all, cond_all, sums = share_small(
        d_modulation,
        cond,
        (first_gain_grad, second_gain_grad, up_bias_grad[0], sums2[4]),
    )
    ada_bias_grad = jnp.sum(d_mod_all, axis=0)
    own_columns = d_mod_all.shape[1] // lax.axis_size("dp")
    mine = lax.dynamic_slice_in_dim(d_mod_all, dp_rank * own_columns, own_columns, axis=1)
    ada_weight_grad = lax.dot_general(
        cond_all, mine, (((0,), (0,)), ((), ())), precision=highest
    )
    d_mod_own = lax.dynamic_slice_in_dim(d_mod_all, dp_rank, 1, axis=0)
    (cond_grad,) = silu_back(jnp.dot(d_mod_own, ada_float.T, precision=highest))
    half = attn_qkv_grad.shape[1] // 2
    qkv_rows = jnp.concatenate(
        [
            scatter_sum(attn_qkv_grad[:, :half], False),
            scatter_sum(attn_qkv_grad[:, half:], True),
        ],
        axis=1,
    )
    return (
        swap_halves(mixed)[None],
        swap_halves(tokens_grad).astype(jnp.float32)[None],
        cond_grad,
        sums[0],
        qkv_rows,
        scatter_sum(attn_out_grad, True),
        sums[1],
        scatter_sum(mlp_up_grad, False),
        sums[2],
        scatter_sum(mlp_down_grad, True),
        sums[3],
        ada_weight_grad,
        ada_bias_grad,
    )


def solution(mesh):
    placed = (
        P("dp", "seq", None),
        P("dp", "seq", None),
        P("dp"),
        P(),
        P(),
        P(),
        P(),
        P(),
        P(),
        P(),
        P(),
        P(),
        P(),
        P(),
    )
    return jax.shard_map(
        per_device,
        mesh=mesh,
        in_specs=placed,
        out_specs=(
            P("dp", "seq", None),
            P("dp", "seq", None),
            P("dp", None),
            P(),
            P("dp", None),
            P("dp", None),
            P(),
            P("dp", None),
            P(),
            P("dp", None),
            P(),
            P(None, "dp"),
            P(),
        ),
        check_vma=False,
    )
```

time: 468 us -> 349 us (0.75); the launches traced: 460 us -> 346 us
  matrix products: 141 us -> 4.79 us
  Pallas kernels: 0 us -> 110 us
  other arithmetic: 94.6 us -> 36.8 us
  local copies, waits for them, and re-layouts: 57.6 us -> 32.1 us
  starting transfers between devices: 68.7 us -> 61.3 us
    dot_general x18 -> x0, matrix products: 136 us -> none  [the longest x4 20.7 us: back_mult(): lax.dot_general(left, right, (((1,), (1,)), ((), ())), preferred_element_...]
    pallas_call x0 -> x10, Pallas kernels: none -> 110 us  [the longest x2 24.5 us: attend_back(): kernel_call(attend_back_body, pairs, [block, block, columns(rows, 128, pa...]
    convert_element_type x7 -> x0, other arithmetic: 29.8 us -> none  [the longest x1 21.9 us: per_device(): d_scores = (probs * (d_probs - delta_sum)).astype(jnp.bfloat16)]
    reduce_sum x9 -> x0, other arithmetic: 23.9 us -> none  [the longest x1 11.1 us: per_device(): totals = jnp.sum(jnp.exp(scores - top_score), axis=-1, keepdims=True)]
    ppermute x5, starting transfers between devices: 32.4 us -> 19.4 us  [swap_halves(): return lax.ppermute(block, ('dp', 'seq'), perm)]
    ppermute x28 -> x27, starting transfers between devices: 27.3 us -> 35.1 us  [swap_bit(): lax.ppermute(block, 'dp', [(i, i ^ bit) for i in range(lax.axis_size('dp'...]
    slice x6 -> x2, local copies, waits for them, and re-layouts: 9.17 us -> 1.8 us  [the longest x1 0.96 us: per_device(): sums2[4]]
    ppermute x28 -> x27, waiting for transfers between devices: 55.3 us -> 62.6 us  [swap_bit(): lax.ppermute(block, 'dp', [(i, i ^ bit) for i in range(lax.axis_size('dp'...]
  transfers between devices with their start and end apart: 42 -> 41, of which waited for: 19 -> 20; matrix products, arithmetic and copies ran while one was open for 30% -> 18% of each run, Pallas kernels for 0% -> 26%
where the time goes in v2:
time: 349 us; the launch traced here: 346 us
  Pallas kernels  110 us (32%)
  waiting for transfers between devices  97 us (28%)
  starting transfers between devices  61.3 us (18%)
  other arithmetic  36.8 us (11%)
  local copies, waits for them, and re-layouts  32.1 us (9%)
  matrix products  4.79 us (1%)
  between operations  4.09 us (1%)
    ppermute x27, waiting for transfers between devices, swap_bit(): lax.ppermute(block, 'dp', [(i, i ^ bit) for i in range(lax.axis_size('dp'...  62.6 us
    ppermute x27, starting transfers between devices, swap_bit(): lax.ppermute(block, 'dp', [(i, i ^ bit) for i in range(lax.axis_size('dp'...  35.1 us
    ppermute x9, waiting for transfers between devices, swap_seq(): return lax.ppermute(block, 'seq', [(0, 1), (1, 0)])  34.4 us
    pallas_call x2, Pallas kernels, attend_back(): kernel_call(attend_back_body, pairs, [block, block, columns(rows, 128, pa...  24.5 us
    ppermute x5, starting transfers between devices, swap_halves(): return lax.ppermute(block, ('dp', 'seq'), perm)  19.4 us
    pallas_call x1, Pallas kernels, down_layer(): kernel_call(down_body, hidden // tile, [columns(rows, tile), columns(rows...  16.8 us
    pallas_call x1, Pallas kernels, up_layer(): kernel_call(up_body, hidden // tile, [block, block, block, full((8, width...  14.7 us
    pallas_call x1, Pallas kernels, attend(): kernel_call(attend_body, pairs, [columns(rows, 128), columns(rows, 128),...  13.5 us
  transfers between devices with their start and end apart: 41, of which 20 were waited for; matrix products, arithmetic and copies ran while one was open for 18% of the time, Pallas kernels for 26%

profile of v2, /device:TPU:0, one launch (start us, length us, event | category | flops | bytes accessed | tf_op | source)
XLA Modules:
  0.0 346.3 jit_solution(17435274684718323510)
XLA Ops:
  0.7 2.0 collective-permute-start.1
  2.7 1.8 collective-permute-start
  12.8 6.9 %shard_map.237 = (bf16[512,768]{1,0:T(8,128)(2,1)}, bf16[512,1536]{1,0:T(8,128)(2,1)}) custom-call(bf16[512,768]{1,0:T(8,128)(2,1)} %copy-done.4, f32[8,768]{1,0:T(8,128)} %pad_maximum_fusion.10.mods, bf16[768,2304]{1,0:T(8,128)(2,1)} %weight.5, f32[512,128]{1,0:T(8,128)} %get-tuple-element.104.cosine, f32[512,128]{1,0:T(8,128)} %get-tuple-element.105.sine), custom_call_target="tpu_custom_call" | custom-call | flops 1207959552 | bytes 4718592 | tf_op jit(solution)/shard_map/pallas_call | solution.py:126
  19.7 7.3 %collective-permute-start.2 = (bf16[512,1536]{1,0:T(8,128)(2,1)}, bf16[512,1536]{1,0:T(8,128)(2,1)}, u32[]{:S(2)}, u32[]{:S(2)}) collective-permute-start(bf16[512,1536]{1,0:T(8,128)(2,1)} %get-tuple-element.43.keys1.values1.keys.values), channel_id=1, source_target_pairs={{0,2},{2,0},{4,6},{6,4},{8,10},{10,8},{12,14},{14,12},{16,18},{18,... | collective-permute-start | bytes 4718600 | tf_op jit(solution)/shard_map/ppermute | solution.py:553
  30.7 4.1 %shard_map.238.query = bf16[512,768]{1,0:T(8,128)(2,1)} custom-call(bf16[512,768]{1,0:T(8,128)(2,1)} %get-tuple-element.42.normed, bf16[768,2304]{1,0:T(8,128)(2,1)} %weight.5, f32[512,128]{1,0:T(8,128)} %get-tuple-element.104.cosine, f32[512,128]{1,0:T(8,128)} %get-tuple-element.105.sine), custom_call_target="tpu_custom_call" | custom-call | flops 603979776 | bytes 2359296 | tf_op jit(solution)/shard_map/pallas_call | solution.py:151
  34.9 13.5 %shard_map.239 = (bf16[512,768]{1,0:T(8,128)(2,1)}, f32[6,2,512]{2,1,0:T(2,128)}) custom-call(bf16[512,768]{1,0:T(8,128)(2,1)} %shard_map.238.query, bf16[512,1536]{1,0:T(8,128)(2,1)} %get-tuple-element.43.keys1.values1.keys.values, bf16[512,1536]{1,0:T(8,128)(2,1)} %get-tuple-element.43.keys1.values1.keys.values, ...), custom_call_target="tpu_custom_call" | custom-call | flops 3221225472 | bytes 3145728 | tf_op jit(solution)/shard_map/pallas_call | solution.py:195
  49.3 14.7 %shard_map.240 = (f32[512,768]{1,0:T(8,128)}, f32[512,768]{1,0:T(8,128)}, bf16[512,768]{1,0:T(8,128)(2,1)}, bf16[512,768]{1,0:T(8,128)(2,1)}, bf16[512,3072]{1,0...) custom-call(bf16[512,768]{1,0:T(8,128)(2,1)} %get-tuple-element.44.attended, ...), custom_call_target="tpu_custom_call" | custom-call | flops 5435817984 | bytes 22020096 | tf_op jit(solution)/shard_map/pallas_call | solution.py:305
  64.0 3.2 dynamic-slice_bitcast_fusion
  68.4 10.5 %shard_map.241 = (bf16[512,3072]{1,0:T(8,128)(2,1)}, bf16[768,3072]{1,0:T(8,128)(2,1)}, f32[1,3072]{1,0:T(1,128)}) custom-call(bf16[512,768]{1,0:T(8,128)(2,1)} %get-tuple-element.46.d_ffn, bf16[512,768]{1,0:T(8,128)(2,1)} %get-tuple-element.47.normed, bf16[3072,768]{1,0:T(8,128)(2,1)} %down_weight.3, bf16[512,3072]{1,0:T(8,128)(2,1)} %get-tuple-element.48.slope), custom_call_target="tpu_custom_call" | custom-call | flops 4831838208 | bytes 22020096 | tf_op jit(solution)/shard_map/pallas_call | solution.py:353
  79.0 16.8 %shard_map.242 = (bf16[512,768]{1,0:T(8,128)(2,1)}, f32[512,768]{1,0:T(8,128)}, bf16[512,768]{1,0:T(8,128)(2,1)}, bf16[768,768]{1,0:T(8,128)(2,1)}, f32[8,768]{1,0:T(8,128)}) custom-call(bf16[512,3072]{1,0:T(8,128)(2,1)} %get-tuple-element.45.activated, bf16[512,3072]{1,0:T(8,128)(2,1)} %get-tuple-element.49.d_pre, bf16[3072,768]{1,0:T(8,128)(2,1)} %down_weight.3, ...), custom_call_target="tpu_custom_call" | custom-call | flops 6039797760 | bytes 15728640 | tf_op jit(solution)/shard_map/pallas_call | solution.py:420
  97.9 7.4 %collective-permute-start.4 = (bf16[512,768]{1,0:T(8,128)(2,1)}, bf16[512,768]{1,0:T(8,128)(2,1)}, u32[]{:S(2)}, u32[]{:S(2)}) collective-permute-start(bf16[512,768]{1,0:T(8,128)(2,1)} %get-tuple-element.52), channel_id=1, source_target_pairs={{0,0},{1,2},{2,1},{3,3},{4,4},{5,6},{6,5},{7,7},{8,8},{9,10},{10,9... | collective-permute-start | bytes 2359304 | tf_op jit(solution)/shard_map/ppermute | solution.py:549
  105.3 12.2 %shard_map.243 = (f32[512,768]{1,0:T(8,128)}, bf16[512,768]{1,0:T(8,128)(2,1)}, bf16[512,768]{1,0:T(8,128)(2,1)}) custom-call(bf16[512,768]{1,0:T(8,128)(2,1)} %shard_map.238.query, bf16[512,1536]{1,0:T(8,128)(2,1)} %collective-permute-done.2.keys2.values2.keys.values, bf16[512,1536]{1,0:T(8,128)(2,1)} %collective-permute-done.2.keys2.values2.keys.values, ...), custom_call_target="tpu_custom_call" | custom-call | flops 4026531840 | bytes 7864320 | tf_op jit(solution)/shard_map/pallas_call | solution.py:248
  118.1 12.3 %shard_map.244 = (f32[512,768]{1,0:T(8,128)}, f32[512,768]{1,0:T(8,128)}, f32[512,768]{1,0:T(8,128)}) custom-call(bf16[512,768]{1,0:T(8,128)(2,1)} %shard_map.238.query, bf16[512,1536]{1,0:T(8,128)(2,1)} %get-tuple-element.43.keys1.values1.keys.values, bf16[512,1536]{1,0:T(8,128)(2,1)} %get-tuple-element.43.keys1.values1.keys.values, ...), custom_call_target="tpu_custom_call" | custom-call | flops 4026531840 | bytes 7864320 | tf_op jit(solution)/shard_map/pallas_call | solution.py:248
  130.4 1.6 dynamic-slice_bitcast_fusion.1
  134.9 2.1 collective-permute-start.25
  137.0 10.1 %shard_map.245 = (bf16[512,2304]{1,0:T(8,128)(2,1)}, bf16[768,2304]{1,0:T(8,128)(2,1)}) custom-call(f32[512,768]{1,0:T(8,128)} %get-tuple-element.56.d_query, f32[512,768]{1,0:T(8,128)} %get-tuple-element.57.d_keys, f32[512,768]{1,0:T(8,128)} %get-tuple-element.58.d_values, bf16[512,768]{1,0:T(8,128)(2,1)} %collective-permute-done.5.peer_keys, ...), custom_call_target="tpu_custom_call" | custom-call | flops 1811939328 | bytes 8650752 | tf_op jit(solution)/shard_map/pallas_call | solution.py:489
  147.1 9.2 %shard_map.246 = (bf16[512,768]{1,0:T(8,128)(2,1)}, f32[8,768]{1,0:T(8,128)}) custom-call(bf16[512,2304]{1,0:T(8,128)(2,1)} %get-tuple-element.61.d_projected, bf16[768,2304]{1,0:T(8,128)(2,1)} %weight.5, bf16[512,768]{1,0:T(8,128)(2,1)} %copy-done.4, f32[512,768]{1,0:T(8,128)} %get-tuple-element.62.d_middle, f32[8,768]{1,0:T(8,128)} %pad_maximum_fusion.10.mods), custom_call_target="tpu_custom_call" | custom-call | flops 1811939328 | bytes 7471104 | tf_op jit(solution)/shard_map/pallas_call | solution.py:533
  157.1 1.3 constant_dynamic-update-slice_fusion.9
  158.4 1.3 constant_dynamic-update-slice_fusion.8
  162.3 1.3 constant_dynamic-update-slice_fusion.5
  164.9 1.3 constant_dynamic-update-slice_fusion.3
  170.1 7.4 %collective-permute-start.7 = (bf16[512,768]{1,0:T(8,128)(2,1)}, bf16[512,768]{1,0:T(8,128)(2,1)}, u32[]{:S(2)}, u32[]{:S(2)}) collective-permute-start(bf16[512,768]{1,0:T(8,128)(2,1)} %get-tuple-element.63), channel_id=1, source_target_pairs={{0,0},{1,2},{2,1},{3,3},{4,4},{5,6},{6,5},{7,7},{8,8},{9,10},{10,9... | collective-permute-start | bytes 2359304 | tf_op jit(solution)/shard_map/ppermute | solution.py:549
  179.4 5.8 %collective-permute-done.9 = f32[10112]{0:T(1024)S(1)} collective-permute-done((f32[10112]{0:T(1024)S(1)}, f32[10112]{0:T(1024)S(1)}, u32[]{:S(2)}, u32[]{:S(2)}) %collective-permute-start.9) | collective-permute-done | bytes 40480 | tf_op jit(solution)/shard_map/ppermute | solution.py:561
  187.1 1.4 reshape.335
  189.3 1.6 collective-permute-start.10
  190.9 1.7 fusion.12
  196.1 1.6 collective-permute-start.11
  197.8 1.6 dynamic-slice_bitcast_fusion.15
  199.3 1.5 collective-permute-done.11
  200.8 1.5 collective-permute-start.26
  203.9 2.3 collective-permute-done.26
  207.2 1.6 collective-permute-start.27
  208.9 2.7 collective-permute-done.27
  212.3 3.0 collective-permute-start.28
  216.1 1.5 collective-permute-done.28
  218.4 3.9 %collective-permute-done.29 = bf16[24,768]{1,0:T(8,128)(2,1)S(1)} collective-permute-done((bf16[24,768]{1,0:T(8,128)(2,1)S(1)}, bf16[24,768]{1,0:T(8,128)(2,1)S(1)}, u32[]{:S(2)}, u32[]{:S(2)}) %collective-permute-start.29) | collective-permute-done | bytes 36896 | tf_op jit(solution)/shard_map/ppermute | solution.py:561
  222.4 3.0 collective-permute-start.12
  226.1 4.6 %collective-permute-done.12 = f32[43264]{0:T(1024)S(1)} collective-permute-done((f32[43264]{0:T(1024)S(1)}, f32[43264]{0:T(1024)S(1)}, u32[]{:S(2)}, u32[]{:S(2)}) %collective-permute-start.12) | collective-permute-done | bytes 173088 | tf_op jit(solution)/shard_map/ppermute | solution.py:553
  235.2 2.4 fusion.36
  237.6 2.5 bitcast_convert_fusion
  240.1 1.4 fusion.5
  241.6 1.6 collective-permute-start.14
  243.2 1.4 fusion.4
  244.7 8.9 %collective-permute-done.14 = bf16[4,1,48,1152]{3,2,0,1:T(8,128)(2,1)S(1)} collective-permute-done((bf16[4,1,48,1152]{3,2,0,1:T(8,128)(2,1)S(1)}, bf16[4,1,48,1152]{3,2,0,1:T(8,128)(2,1)S(1)}, u32[]{:S(2)}, u32[]{:S(2)}) %collective-permute-start.14) | collective-permute-done | bytes 442400 | tf_op jit(solution)/shard_map/ppermute | solution.py:553
  254.8 1.5 collective-permute-done.19
  257.1 3.0 collective-permute-done.15
  260.2 2.7 collective-permute-start.16
  263.0 1.8 collective-permute-start.21
  264.8 2.2 fusion
  267.3 2.6 fusion.1
  269.9 2.9 collective-permute-start.22
  273.5 2.1 collective-permute-done.22
  275.6 1.9 collective-permute-start.23
  277.8 17.2 %collective-permute-done.23 = bf16[24,1152]{1,0:T(8,128)(2,1)S(1)} collective-permute-done((bf16[24,1152]{1,0:T(8,128)(2,1)S(1)}, bf16[24,1152]{1,0:T(8,128)(2,1)S(1)}, u32[]{:S(2)}, u32[]{:S(2)}) %collective-permute-start.23) | collective-permute-done | bytes 55328 | tf_op jit(solution)/shard_map/ppermute | solution.py:561
  295.4 1.6 collective-permute-start.37
  297.0 4.9 %collective-permute-done.31 = bf16[4,1,48,3072]{3,2,0,1:T(8,128)(2,1)S(1)} collective-permute-done((bf16[4,1,48,3072]{3,2,0,1:T(8,128)(2,1)S(1)}, bf16[4,1,48,3072]{3,2,0,1:T(8,128)(2,1)S(1)}, u32[]{:S(2)}, u32[]{:S(2)}) %collective-permute-start.31) | collective-permute-done | bytes 1179680 | tf_op jit(solution)/shard_map/ppermute | solution.py:553
  302.5 8.2 %collective-permute-done.37 = bf16[4,1,96,768]{3,2,0,1:T(8,128)(2,1)S(1)} collective-permute-done((bf16[4,1,96,768]{3,2,0,1:T(8,128)(2,1)S(1)}, bf16[4,1,96,768]{3,2,0,1:T(8,128)(2,1)S(1)}, u32[]{:S(2)}, u32[]{:S(2)}) %collective-permute-start.37) | collective-permute-done | bytes 589856 | tf_op jit(solution)/shard_map/ppermute | solution.py:553
  311.3 6.5 %collective-permute-done.32 = bf16[2,1,48,3072]{3,2,0,1:T(8,128)(2,1)S(1)} collective-permute-done((bf16[2,1,48,3072]{3,2,0,1:T(8,128)(2,1)S(1)}, bf16[2,1,48,3072]{3,2,0,1:T(8,128)(2,1)S(1)}, u32[]{:S(2)}, u32[]{:S(2)}) %collective-permute-start.32) | collective-permute-done | bytes 589856 | tf_op jit(solution)/shard_map/ppermute | solution.py:553
  318.1 3.7 %collective-permute-done.38 = bf16[2,1,96,768]{3,2,0,1:T(8,128)(2,1)S(1)} collective-permute-done((bf16[2,1,96,768]{3,2,0,1:T(8,128)(2,1)S(1)}, bf16[2,1,96,768]{3,2,0,1:T(8,128)(2,1)S(1)}, u32[]{:S(2)}, u32[]{:S(2)}) %collective-permute-start.38) | collective-permute-done | bytes 294944 | tf_op jit(solution)/shard_map/ppermute | solution.py:553
  322.8 11.4 %collective-permute-done.39 = bf16[1,1,96,768]{3,2,0,1:T(8,128)(2,1)S(1)} collective-permute-done((bf16[1,1,96,768]{3,2,0,1:T(8,128)(2,1)S(1)}, bf16[1,1,96,768]{3,2,0,1:T(8,128)(2,1)S(1)}, u32[]{:S(2)}, u32[]{:S(2)}) %collective-permute-start.39) | collective-permute-done | bytes 147488 | tf_op jit(solution)/shard_map/ppermute | solution.py:553
  334.2 1.4 collective-permute-start.40
  336.5 3.8 %collective-permute-done.40 = bf16[96,768]{1,0:T(8,128)(2,1)S(1)} collective-permute-done((bf16[96,768]{1,0:T(8,128)(2,1)S(1)}, bf16[96,768]{1,0:T(8,128)(2,1)S(1)}, u32[]{:S(2)}, u32[]{:S(2)}) %collective-permute-start.40) | collective-permute-done | bytes 147488 | tf_op jit(solution)/shard_map/ppermute | solution.py:561
  341.1 2.3 collective-permute-done.34
  344.3 2.1 copy.68
  (205 shorter events, 52.7 us)
Async XLA Ops:
  0.6 9.4 %copy-start = (bf16[128,4608]{1,0:T(8,128)(2,1)S(1)}, bf16[128,4608]{1,0:T(8,128)(2,1)}, u32[]{:S(2)}) copy-start(bf16[128,4608]{1,0:T(8,128)(2,1)} %param.26) | copy-start | bytes 3538948
  0.7 10.6 %copy-start.15 = (bf16[4608]{0:T(1024)(128)(2,1)S(1)}, bf16[4608]{0:T(1024)(128)(2,1)}, u32[]{:S(2)}) copy-start(bf16[4608]{0:T(1024)(128)(2,1)} %param.27) | copy-start | bytes 27652
  0.7 7.4 %collective-permute-start.1 = (s32[1]{0:T(128)}, s32[1]{0:T(128)}, u32[]{:S(2)}, u32[]{:S(2)}) collective-permute-start(s32[1]{0:T(128)} %param.16), channel_id=1, source_target_pairs={{0,0},{1,2},{2,1},{3,3},{4,4},{5,6},{6,5},{7,7},{8,8},{9,10},{10,9... | collective-permute-start | bytes 20 | tf_op jit(solution)/shard_map/ppermute | solution.py:549
  2.7 9.3 %collective-permute-start = (bf16[512,768]{1,0:T(8,128)(2,1)}, bf16[512,768]{1,0:T(8,128)(2,1)S(1)}, u32[]{:S(2)}, u32[]{:S(2)}) collective-permute-start(bf16[512,768]{1,0:T(8,128)(2,1)} %bitcast.200), channel_id=1, source_target_pairs={{0,0},{1,2},{2,1},{3,3},{4,4},{5,6},{6,5},{7,7},{8,8},{9,10},{10,9... | collective-permute-start | bytes 2359304 | tf_op jit(solution)/shard_map/ppermute | solution.py:549
  12.0 0.9 copy-start.4
  12.8 14.2 %copy-start.20 = (bf16[1,512,768]{2,1,0:T(8,128)(2,1)S(1)}, bf16[1,512,768]{2,1,0:T(8,128)(2,1)}, u32[]{:S(2)}) copy-start(bf16[1,512,768]{2,1,0:T(8,128)(2,1)} %param.15) | copy-start | bytes 2359300
  12.8 15.9 %copy-start.19 = (bf16[768]{0:T(1024)(128)(2,1)S(1)}, bf16[768]{0:T(1024)(128)(2,1)}, u32[]{:S(2)}) copy-start(bf16[768]{0:T(1024)(128)(2,1)} %param.25) | copy-start | bytes 4612
  12.8 16.5 %copy-start.18 = (bf16[3072]{0:T(1024)(128)(2,1)S(1)}, bf16[3072]{0:T(1024)(128)(2,1)}, u32[]{:S(2)}) copy-start(bf16[3072]{0:T(1024)(128)(2,1)} %param.23) | copy-start | bytes 18436
  19.7 15.1 %collective-permute-start.2 = (bf16[512,1536]{1,0:T(8,128)(2,1)}, bf16[512,1536]{1,0:T(8,128)(2,1)}, u32[]{:S(2)}, u32[]{:S(2)}) collective-permute-start(bf16[512,1536]{1,0:T(8,128)(2,1)} %get-tuple-element.43.keys1.values1.keys.values), channel_id=1, source_target_pairs={{0,2},{2,0},{4,6},{6,4},{8,10},{10,8},{12,14},{14,12},{16,18},{18,... | collective-permute-start | bytes 4718600 | tf_op jit(solution)/shard_map/ppermute | solution.py:553
  27.1 21.3 %collective-permute-start.3 = (bf16[512,768]{1,0:T(8,128)(2,1)S(1)}, bf16[512,768]{1,0:T(8,128)(2,1)S(1)}, u32[]{:S(2)}, u32[]{:S(2)}) collective-permute-start(bf16[512,768]{1,0:T(8,128)(2,1)S(1)} %bitcast.201), channel_id=1, source_target_pairs={{0,0},{1,2},{2,1},{3,3},{4,4},{5,6},{6,5},{7,7},{8,8},{9,10},{10,9... | collective-permute-start | bytes 2359304 | tf_op jit(solution)/shard_map/ppermute | solution.py:549
  48.4 0.9 copy-start.7
  67.2 197.6 %collective-permute-start.35 = (bf16[8,1,192,768]{3,2,0,1:T(8,128)(2,1)}, bf16[8,1,192,768]{3,2,0,1:T(8,128)(2,1)}, u32[]{:S(2)}, u32[]{:S(2)}) collective-permute-start(bf16[8,1,192,768]{3,2,0,1:T(8,128)(2,1)} %dynamic-slice_bitcast_fusion), channel_id=1, source_target_pairs={{0,2},{2,0},{4,6},{6,4},{8,10},{10,8},{12,14},{14,12},{16,18},{18,... | collective-permute-start | bytes 7077896 | tf_op jit(solution)/shard_map/ppermute | solution.py:553
  97.8 34.3 %collective-permute-start.24 = (bf16[8,1,48,768]{3,2,0,1:T(8,128)(2,1)S(1)}, bf16[8,1,48,768]{3,2,0,1:T(8,128)(2,1)S(1)}, u32[]{:S(2)}, u32[]{:S(2)}) collective-permute-start(bf16[8,1,48,768]{3,2,0,1:T(8,128)(2,1)S(1)} %dynamic-slice_bitcast_fusion.8), channel_id=1, source_target_pairs={{0,2},{2,0},{4,6},{6,4},{8,10},{10,8},{12,14},{14,12},{16,18},{18,... | collective-permute-start | bytes 1769480 | tf_op jit(solution)/shard_map/ppermute | solution.py:553
  97.9 72.2 %collective-permute-start.4 = (bf16[512,768]{1,0:T(8,128)(2,1)}, bf16[512,768]{1,0:T(8,128)(2,1)}, u32[]{:S(2)}, u32[]{:S(2)}) collective-permute-start(bf16[512,768]{1,0:T(8,128)(2,1)} %get-tuple-element.52), channel_id=1, source_target_pairs={{0,0},{1,2},{2,1},{3,3},{4,4},{5,6},{6,5},{7,7},{8,8},{9,10},{10,9... | collective-permute-start | bytes 2359304 | tf_op jit(solution)/shard_map/ppermute | solution.py:549
  105.3 25.1 %slice-start = ((s8[4718592]{0:T(1024)(128)(4,1)}), s8[4194304]{0:T(1024)(128)(4,1)S(1)}, s32[]{:S(2)}) async-start(s8[4718592]{0:T(1024)(128)(4,1)} %bitcast.164), calls=%async_computation | async-start | bytes 8388608
  117.5 17.4 %collective-permute-start.5 = (bf16[512,768]{1,0:T(8,128)(2,1)}, bf16[512,768]{1,0:T(8,128)(2,1)}, u32[]{:S(2)}, u32[]{:S(2)}) collective-permute-start(bf16[512,768]{1,0:T(8,128)(2,1)} %get-tuple-element.59), channel_id=1, source_target_pairs={{0,2},{2,0},{4,6},{6,4},{8,10},{10,8},{12,14},{14,12},{16,18},{18,... | collective-permute-start | bytes 2359304 | tf_op jit(solution)/shard_map/ppermute | solution.py:553
  117.6 12.8 %slice-start.1 = ((s8[4718592]{0:T(1024)(128)(4,1)}), s8[524288]{0:T(1024)(128)(4,1)S(1)}, s32[]{:S(2)}) async-start(s8[4718592]{0:T(1024)(128)(4,1)} %bitcast.164), calls=%async_computation.1 | async-start | bytes 1048576
  117.6 19.4 %collective-permute-start.6 = (bf16[512,768]{1,0:T(8,128)(2,1)}, bf16[512,768]{1,0:T(8,128)(2,1)}, u32[]{:S(2)}, u32[]{:S(2)}) collective-permute-start(bf16[512,768]{1,0:T(8,128)(2,1)} %get-tuple-element.60), channel_id=1, source_target_pairs={{0,2},{2,0},{4,6},{6,4},{8,10},{10,8},{12,14},{14,12},{16,18},{18,... | collective-permute-start | bytes 2359304 | tf_op jit(solution)/shard_map/ppermute | solution.py:553
  130.4 2.5 copy-start.6
  132.1 0.8 copy-start.8
  132.9 134.4 %collective-permute-start.30 = (bf16[8,1,48,3072]{3,2,0,1:T(8,128)(2,1)}, bf16[8,1,48,3072]{3,2,0,1:T(8,128)(2,1)}, u32[]{:S(2)}, u32[]{:S(2)}) collective-permute-start(bf16[8,1,48,3072]{3,2,0,1:T(8,128)(2,1)} %dynamic-slice_bitcast_fusion.1), channel_id=1, source_target_pairs={{0,2},{2,0},{4,6},{6,4},{8,10},{10,8},{12,14},{14,12},{16,18},{18,... | collective-permute-start | bytes 7077896 | tf_op jit(solution)/shard_map/ppermute | solution.py:553
  134.9 54.5 %collective-permute-start.25 = (bf16[8,24,768]{2,1,0:T(8,128)(2,1)}, bf16[8,24,768]{2,1,0:T(8,128)(2,1)}, u32[]{:S(2)}, u32[]{:S(2)}) collective-permute-start(bf16[8,24,768]{2,1,0:T(8,128)(2,1)} %dynamic-slice_bitcast_fusion.12), channel_id=1, source_target_pairs={{0,1},{1,0},{2,3},{3,2},{4,5},{5,4},{6,7},{7,6},{8,9},{9,8},{10,11... | collective-permute-start | bytes 884744 | tf_op jit(solution)/shard_map/ppermute | solution.py:561
  147.0 11.4 %copy-start.16 = (bf16[768]{0:T(1024)(128)(2,1)S(1)}, bf16[768]{0:T(1024)(128)(2,1)}, u32[]{:S(2)}) copy-start(bf16[768]{0:T(1024)(128)(2,1)} %param.18) | copy-start | bytes 4612
  147.0 15.3 %copy-start.17 = (bf16[768]{0:T(1024)(128)(2,1)S(1)}, bf16[768]{0:T(1024)(128)(2,1)}, u32[]{:S(2)}) copy-start(bf16[768]{0:T(1024)(128)(2,1)} %param.21) | copy-start | bytes 4612
  147.1 20.5 %copy-start.14 = (f32[1,3072]{1,0:T(1,128)S(1)}, f32[1,3072]{1,0:T(1,128)}, u32[]{:S(2)}) copy-start(f32[1,3072]{1,0:T(1,128)} %get-tuple-element.66) | copy-start | bytes 36868
  147.1 21.6 %copy-start.3 = (bf16[768,2304]{1,0:T(8,128)(2,1)S(1)}, bf16[768,2304]{1,0:T(8,128)(2,1)}, u32[]{:S(2)}) copy-start(bf16[768,2304]{1,0:T(8,128)(2,1)} %get-tuple-element.67) | copy-start | bytes 10616836
  168.7 8.8 %collective-permute-start.8 = (f32[9984]{0:T(1024)}, f32[9984]{0:T(1024)S(1)}, u32[]{:S(2)}, u32[]{:S(2)}) collective-permute-start(f32[9984]{0:T(1024)} %constant_dynamic-update-slice_fusion), channel_id=1, source_target_pairs={{0,2},{2,0},{4,6},{6,4},{8,10},{10,8},{12,14},{14,12},{16,18},{18,... | collective-permute-start | bytes 119816 | tf_op jit(solution)/shard_map/ppermute | solution.py:553
  169.0 10.4 %copy-start.1 = (bf16[768,1152]{1,0:T(8,128)(2,1)}, bf16[768,1152]{1,0:T(8,128)(2,1)S(1)}, u32[]{:S(2)}) copy-start(bf16[768,1152]{1,0:T(8,128)(2,1)S(1)} %get-tuple-element.82) | copy-start | bytes 5308420
  170.1 67.5 %collective-permute-start.7 = (bf16[512,768]{1,0:T(8,128)(2,1)}, bf16[512,768]{1,0:T(8,128)(2,1)}, u32[]{:S(2)}, u32[]{:S(2)}) collective-permute-start(bf16[512,768]{1,0:T(8,128)(2,1)} %get-tuple-element.63), channel_id=1, source_target_pairs={{0,0},{1,2},{2,1},{3,3},{4,4},{5,6},{6,5},{7,7},{8,8},{9,10},{10,9... | collective-permute-start | bytes 2359304 | tf_op jit(solution)/shard_map/ppermute | solution.py:549
  178.3 6.9 %collective-permute-start.9 = (f32[10112]{0:T(1024)S(1)}, f32[10112]{0:T(1024)S(1)}, u32[]{:S(2)}, u32[]{:S(2)}) collective-permute-start(f32[10112]{0:T(1024)S(1)} %pad_maximum_fusion.8), channel_id=1, source_target_pairs={{0,1},{1,0},{2,3},{3,2},{4,5},{5,4},{6,7},{7,6},{8,9},{9,8},{10,11... | collective-permute-start | bytes 121352 | tf_op jit(solution)/shard_map/ppermute | solution.py:561
  185.2 55.0 %collective-permute-start.13 = (bf16[8,1,48,1152]{3,2,0,1:T(8,128)(2,1)}, bf16[8,1,48,1152]{3,2,0,1:T(8,128)(2,1)}, u32[]{:S(2)}, u32[]{:S(2)}) collective-permute-start(bf16[8,1,48,1152]{3,2,0,1:T(8,128)(2,1)} %dynamic-slice_bitcast_fusion.5), channel_id=1, source_target_pairs={{0,2},{2,0},{4,6},{6,4},{8,10},{10,8},{12,14},{14,12},{16,18},{18,... | collective-permute-start | bytes 2654216 | tf_op jit(solution)/shard_map/ppermute | solution.py:553
  189.3 4.5 %collective-permute-start.10 = (f32[14848]{0:T(1024)S(1)}, f32[14848]{0:T(1024)S(1)}, u32[]{:S(2)}, u32[]{:S(2)}) collective-permute-start(f32[14848]{0:T(1024)S(1)} %pad_maximum_fusion.7), channel_id=1, source_target_pairs={{0,4},{2,6},{4,0},{6,2},{8,12},{10,14},{12,8},{14,10},{16,20},{18,... | collective-permute-start | bytes 178184 | tf_op jit(solution)/shard_map/ppermute | solution.py:553
  192.7 13.6 %copy-start.5 = (bf16[8,24,768]{2,1,0:T(8,128)(2,1)S(1)}, bf16[8,24,768]{2,1,0:T(8,128)(2,1)}, u32[]{:S(2)}) copy-start(bf16[8,24,768]{2,1,0:T(8,128)(2,1)} %fusion.12) | copy-start | bytes 884740
  196.1 4.7 %collective-permute-start.11 = (f32[24320]{0:T(1024)S(1)}, f32[24320]{0:T(1024)S(1)}, u32[]{:S(2)}, u32[]{:S(2)}) collective-permute-start(f32[24320]{0:T(1024)S(1)} %pad_maximum_fusion.5), channel_id=1, source_target_pairs={{0,8},{2,10},{4,12},{6,14},{8,0},{10,2},{12,4},{14,6},{16,24},{18,... | collective-permute-start | bytes 291848 | tf_op jit(solution)/shard_map/ppermute | solution.py:553
  200.8 1.5 copy-start.12
  200.8 5.5 %collective-permute-start.26 = (bf16[4,1,24,768]{3,2,0,1:T(8,128)(2,1)}, bf16[4,1,24,768]{3,2,0,1:T(8,128)(2,1)}, u32[]{:S(2)}, u32[]{:S(2)}) collective-permute-start(bf16[4,1,24,768]{3,2,0,1:T(8,128)(2,1)} %dynamic-slice_bitcast_fusion.15), channel_id=1, source_target_pairs={{0,4},{2,6},{4,0},{6,2},{8,12},{10,14},{12,8},{14,10},{16,20},{18,... | collective-permute-start | bytes 442376 | tf_op jit(solution)/shard_map/ppermute | solution.py:553
  207.2 4.4 %collective-permute-start.27 = (bf16[2,1,24,768]{3,2,0,1:T(8,128)(2,1)S(1)}, bf16[2,1,24,768]{3,2,0,1:T(8,128)(2,1)S(1)}, u32[]{:S(2)}, u32[]{:S(2)}) collective-permute-start(bf16[2,1,24,768]{3,2,0,1:T(8,128)(2,1)S(1)} %dynamic-slice_bitcast_fusion.17), channel_id=1, source_target_pairs={{0,8},{2,10},{4,12},{6,14},{8,0},{10,2},{12,4},{14,6},{16,24},{18,... | collective-permute-start | bytes 221192 | tf_op jit(solution)/shard_map/ppermute | solution.py:553
  212.3 5.2 %collective-permute-start.28 = (bf16[1,1,24,768]{3,2,0,1:T(8,128)(2,1)}, bf16[1,1,24,768]{3,2,0,1:T(8,128)(2,1)}, u32[]{:S(2)}, u32[]{:S(2)}) collective-permute-start(bf16[1,1,24,768]{3,2,0,1:T(8,128)(2,1)} %constant_dynamic-slice_fusion.2), channel_id=1, source_target_pairs={{0,16},{2,18},{4,20},{6,22},{8,24},{10,26},{12,28},{14,30},{16,0},... | collective-permute-start | bytes 110600 | tf_op jit(solution)/shard_map/ppermute | solution.py:553
  218.3 4.0 %collective-permute-start.29 = (bf16[24,768]{1,0:T(8,128)(2,1)S(1)}, bf16[24,768]{1,0:T(8,128)(2,1)S(1)}, u32[]{:S(2)}, u32[]{:S(2)}) collective-permute-start(bf16[24,768]{1,0:T(8,128)(2,1)S(1)} %fusion.24), channel_id=1, source_target_pairs={{0,1},{1,0},{2,3},{3,2},{4,5},{5,4},{6,7},{7,6},{8,9},{9,8},{10,11... | collective-permute-start | bytes 110600 | tf_op jit(solution)/shard_map/ppermute | solution.py:561
  222.4 8.3 %collective-permute-start.12 = (f32[43264]{0:T(1024)S(1)}, f32[43264]{0:T(1024)S(1)}, u32[]{:S(2)}, u32[]{:S(2)}) collective-permute-start(f32[43264]{0:T(1024)S(1)} %pad_maximum_fusion.3), channel_id=1, source_target_pairs={{0,16},{2,18},{4,20},{6,22},{8,24},{10,26},{12,28},{14,30},{16,0},... | collective-permute-start | bytes 519176 | tf_op jit(solution)/shard_map/ppermute | solution.py:553
  230.7 12.5 %collective-permute-start.18 = (bf16[8,1,48,1152]{3,2,0,1:T(8,128)(2,1)}, bf16[8,1,48,1152]{3,2,0,1:T(8,128)(2,1)}, u32[]{:S(2)}, u32[]{:S(2)}) collective-permute-start(bf16[8,1,48,1152]{3,2,0,1:T(8,128)(2,1)} %dynamic-slice_bitcast_fusion.4), channel_id=1, source_target_pairs={{0,2},{2,0},{4,6},{6,4},{8,10},{10,8},{12,14},{14,12},{16,18},{18,... | collective-permute-start | bytes 2654216 | tf_op jit(solution)/shard_map/ppermute | solution.py:553
  235.2 4.9 %copy-start.2 = (bf16[768,1152]{1,0:T(8,128)(2,1)S(1)}, bf16[768,1152]{1,0:T(8,128)(2,1)}, u32[]{:S(2)}) copy-start(bf16[768,1152]{1,0:T(8,128)(2,1)} %copy-done.1) | copy-start | bytes 5308420
  237.6 27.2 %slice-start.4 = ((s8[4718592]{0:T(1024)(128)(4,1)}), s8[4194304]{0:T(1024)(128)(4,1)S(1)}, s32[]{:S(2)}) async-start(s8[4718592]{0:T(1024)(128)(4,1)} %bitcast.171), calls=%async_computation.4 | async-start | bytes 8388608
  241.6 23.2 %slice-start.5 = ((s8[4718592]{0:T(1024)(128)(4,1)}), s8[524288]{0:T(1024)(128)(4,1)S(1)}, s32[]{:S(2)}) async-start(s8[4718592]{0:T(1024)(128)(4,1)} %bitcast.171), calls=%async_computation.5 | async-start | bytes 1048576
  241.6 12.0 %collective-permute-start.14 = (bf16[4,1,48,1152]{3,2,0,1:T(8,128)(2,1)S(1)}, bf16[4,1,48,1152]{3,2,0,1:T(8,128)(2,1)S(1)}, u32[]{:S(2)}, u32[]{:S(2)}) collective-permute-start(bf16[4,1,48,1152]{3,2,0,1:T(8,128)(2,1)S(1)} %dynamic-slice_bitcast_fusion.10), channel_id=1, source_target_pairs={{0,4},{2,6},{4,0},{6,2},{8,12},{10,14},{12,8},{14,10},{16,20},{18,... | collective-permute-start | bytes 1327112 | tf_op jit(solution)/shard_map/ppermute | solution.py:553
  244.6 11.7 %collective-permute-start.19 = (bf16[8,24,1152]{2,1,0:T(8,128)(2,1)S(1)}, bf16[8,24,1152]{2,1,0:T(8,128)(2,1)S(1)}, u32[]{:S(2)}, u32[]{:S(2)}) collective-permute-start(bf16[8,24,1152]{2,1,0:T(8,128)(2,1)S(1)} %dynamic-slice_bitcast_fusion.9), channel_id=1, source_target_pairs={{0,1},{1,0},{2,3},{3,2},{4,5},{5,4},{6,7},{7,6},{8,9},{9,8},{10,11... | collective-permute-start | bytes 1327112 | tf_op jit(solution)/shard_map/ppermute | solution.py:561
  253.7 6.4 %collective-permute-start.15 = (bf16[2,1,48,1152]{3,2,0,1:T(8,128)(2,1)S(1)}, bf16[2,1,48,1152]{3,2,0,1:T(8,128)(2,1)S(1)}, u32[]{:S(2)}, u32[]{:S(2)}) collective-permute-start(bf16[2,1,48,1152]{3,2,0,1:T(8,128)(2,1)S(1)} %dynamic-slice_bitcast_fusion.14), channel_id=1, source_target_pairs={{0,8},{2,10},{4,12},{6,14},{8,0},{10,2},{12,4},{14,6},{16,24},{18,... | collective-permute-start | bytes 663560 | tf_op jit(solution)/shard_map/ppermute | solution.py:553
  256.5 6.4 %collective-permute-start.20 = (bf16[4,1,24,1152]{3,2,0,1:T(8,128)(2,1)S(1)}, bf16[4,1,24,1152]{3,2,0,1:T(8,128)(2,1)S(1)}, u32[]{:S(2)}, u32[]{:S(2)}) collective-permute-start(bf16[4,1,24,1152]{3,2,0,1:T(8,128)(2,1)S(1)} %dynamic-slice_bitcast_fusion.13), channel_id=1, source_target_pairs={{0,4},{2,6},{4,0},{6,2},{8,12},{10,14},{12,8},{14,10},{16,20},{18,... | collective-permute-start | bytes 663560 | tf_op jit(solution)/shard_map/ppermute | solution.py:553
  260.1 7.2 %slice-start.2 = ((s8[4718592]{0:T(1024)(128)(4,1)}), s8[4194304]{0:T(1024)(128)(4,1)S(1)}, s32[]{:S(2)}) async-start(s8[4718592]{0:T(1024)(128)(4,1)} %bitcast.167), calls=%async_computation.2 | async-start | bytes 8388608
  260.2 17.3 %collective-permute-start.16 = (bf16[1,1,48,1152]{3,2,0,1:T(8,128)(2,1)S(1)}, bf16[1,1,48,1152]{3,2,0,1:T(8,128)(2,1)S(1)}, u32[]{:S(2)}, u32[]{:S(2)}) collective-permute-start(bf16[1,1,48,1152]{3,2,0,1:T(8,128)(2,1)S(1)} %constant_dynamic-slice_fusion.4), channel_id=1, source_target_pairs={{0,16},{2,18},{4,20},{6,22},{8,24},{10,26},{12,28},{14,30},{16,0},... | collective-permute-start | bytes 331784 | tf_op jit(solution)/shard_map/ppermute | solution.py:553
  263.0 4.3 %slice-start.3 = ((s8[4718592]{0:T(1024)(128)(4,1)}), s8[524288]{0:T(1024)(128)(4,1)S(1)}, s32[]{:S(2)}) async-start(s8[4718592]{0:T(1024)(128)(4,1)} %bitcast.167), calls=%async_computation.3 | async-start | bytes 1048576
  263.0 6.9 %collective-permute-start.21 = (bf16[2,1,24,1152]{3,2,1,0:T(8,128)(2,1)S(1)}, bf16[2,1,24,1152]{3,2,1,0:T(8,128)(2,1)S(1)}, u32[]{:S(2)}, u32[]{:S(2)}) collective-permute-start(bf16[2,1,24,1152]{3,2,1,0:T(8,128)(2,1)S(1)} %dynamic-slice_bitcast_fusion.16), channel_id=1, source_target_pairs={{0,8},{2,10},{4,12},{6,14},{8,0},{10,2},{12,4},{14,6},{16,24},{18,... | collective-permute-start | bytes 331784 | tf_op jit(solution)/shard_map/ppermute | solution.py:553
  267.2 27.8 %collective-permute-start.36 = (bf16[8,96,768]{2,1,0:T(8,128)(2,1)S(1)}, bf16[8,96,768]{2,1,0:T(8,128)(2,1)S(1)}, u32[]{:S(2)}, u32[]{:S(2)}) collective-permute-start(bf16[8,96,768]{2,1,0:T(8,128)(2,1)S(1)} %dynamic-slice_bitcast_fusion.2), channel_id=1, source_target_pairs={{0,1},{1,0},{2,3},{3,2},{4,5},{5,4},{6,7},{7,6},{8,9},{9,8},{10,11... | collective-permute-start | bytes 3538952 | tf_op jit(solution)/shard_map/ppermute | solution.py:561
  269.9 5.6 %collective-permute-start.22 = (bf16[1,1,24,1152]{3,2,1,0:T(8,128)(2,1)S(1)}, bf16[1,1,24,1152]{3,2,1,0:T(8,128)(2,1)S(1)}, u32[]{:S(2)}, u32[]{:S(2)}) collective-permute-start(bf16[1,1,24,1152]{3,2,1,0:T(8,128)(2,1)S(1)} %constant_dynamic-slice_fusion.3), channel_id=1, source_target_pairs={{0,16},{2,18},{4,20},{6,22},{8,24},{10,26},{12,28},{14,30},{16,0},... | collective-permute-start | bytes 165896 | tf_op jit(solution)/shard_map/ppermute | solution.py:553
  272.9 29.0 %collective-permute-start.31 = (bf16[4,1,48,3072]{3,2,0,1:T(8,128)(2,1)S(1)}, bf16[4,1,48,3072]{3,2,0,1:T(8,128)(2,1)S(1)}, u32[]{:S(2)}, u32[]{:S(2)}) collective-permute-start(bf16[4,1,48,3072]{3,2,0,1:T(8,128)(2,1)S(1)} %dynamic-slice_bitcast_fusion.3), channel_id=1, source_target_pairs={{0,4},{2,6},{4,0},{6,2},{8,12},{10,14},{12,8},{14,10},{16,20},{18,... | collective-permute-start | bytes 3538952 | tf_op jit(solution)/shard_map/ppermute | solution.py:553
  275.6 19.4 %collective-permute-start.23 = (bf16[24,1152]{1,0:T(8,128)(2,1)S(1)}, bf16[24,1152]{1,0:T(8,128)(2,1)S(1)}, u32[]{:S(2)}, u32[]{:S(2)}) collective-permute-start(bf16[24,1152]{1,0:T(8,128)(2,1)S(1)} %fusion.23), channel_id=1, source_target_pairs={{0,1},{1,0},{2,3},{3,2},{4,5},{5,4},{6,7},{7,6},{8,9},{9,8},{10,11... | collective-permute-start | bytes 165896 | tf_op jit(solution)/shard_map/ppermute | solution.py:561
  277.5 25.0 %collective-permute-start.17 = (bf16[48,1152]{1,0:T(8,128)(2,1)S(1)}, bf16[48,1152]{1,0:T(8,128)(2,1)S(1)}, u32[]{:S(2)}, u32[]{:S(2)}) collective-permute-start(bf16[48,1152]{1,0:T(8,128)(2,1)S(1)} %fusion.21), channel_id=1, source_target_pairs={{0,1},{1,0},{2,3},{3,2},{4,5},{5,4},{6,7},{7,6},{8,9},{9,8},{10,11... | collective-permute-start | bytes 331784 | tf_op jit(solution)/shard_map/ppermute | solution.py:561
  295.4 15.3 %collective-permute-start.37 = (bf16[4,1,96,768]{3,2,0,1:T(8,128)(2,1)S(1)}, bf16[4,1,96,768]{3,2,0,1:T(8,128)(2,1)S(1)}, u32[]{:S(2)}, u32[]{:S(2)}) collective-permute-start(bf16[4,1,96,768]{3,2,0,1:T(8,128)(2,1)S(1)} %dynamic-slice_bitcast_fusion.6), channel_id=1, source_target_pairs={{0,4},{2,6},{4,0},{6,2},{8,12},{10,14},{12,8},{14,10},{16,20},{18,... | collective-permute-start | bytes 1769480 | tf_op jit(solution)/shard_map/ppermute | solution.py:553
  302.4 15.5 %collective-permute-start.32 = (bf16[2,1,48,3072]{3,2,0,1:T(8,128)(2,1)S(1)}, bf16[2,1,48,3072]{3,2,0,1:T(8,128)(2,1)S(1)}, u32[]{:S(2)}, u32[]{:S(2)}) collective-permute-start(bf16[2,1,48,3072]{3,2,0,1:T(8,128)(2,1)S(1)} %dynamic-slice_bitcast_fusion.7), channel_id=1, source_target_pairs={{0,8},{2,10},{4,12},{6,14},{8,0},{10,2},{12,4},{14,6},{16,24},{18,... | collective-permute-start | bytes 1769480 | tf_op jit(solution)/shard_map/ppermute | solution.py:553
  310.9 10.9 %collective-permute-start.38 = (bf16[2,1,96,768]{3,2,0,1:T(8,128)(2,1)S(1)}, bf16[2,1,96,768]{3,2,0,1:T(8,128)(2,1)S(1)}, u32[]{:S(2)}, u32[]{:S(2)}) collective-permute-start(bf16[2,1,96,768]{3,2,0,1:T(8,128)(2,1)S(1)} %dynamic-slice_bitcast_fusion.11), channel_id=1, source_target_pairs={{0,8},{2,10},{4,12},{6,14},{8,0},{10,2},{12,4},{14,6},{16,24},{18,... | collective-permute-start | bytes 884744 | tf_op jit(solution)/shard_map/ppermute | solution.py:553
  318.0 17.5 %collective-permute-start.33 = (bf16[1,1,48,3072]{3,2,0,1:T(8,128)(2,1)S(1)}, bf16[1,1,48,3072]{3,2,0,1:T(8,128)(2,1)S(1)}, u32[]{:S(2)}, u32[]{:S(2)}) collective-permute-start(bf16[1,1,48,3072]{3,2,0,1:T(8,128)(2,1)S(1)} %constant_dynamic-slice_fusion.1), channel_id=1, source_target_pairs={{0,16},{2,18},{4,20},{6,22},{8,24},{10,26},{12,28},{14,30},{16,0},... | collective-permute-start | bytes 884744 | tf_op jit(solution)/shard_map/ppermute | solution.py:553
  321.9 12.3 %collective-permute-start.39 = (bf16[1,1,96,768]{3,2,0,1:T(8,128)(2,1)S(1)}, bf16[1,1,96,768]{3,2,0,1:T(8,128)(2,1)S(1)}, u32[]{:S(2)}, u32[]{:S(2)}) collective-permute-start(bf16[1,1,96,768]{3,2,0,1:T(8,128)(2,1)S(1)} %constant_dynamic-slice_fusion), channel_id=1, source_target_pairs={{0,16},{2,18},{4,20},{6,22},{8,24},{10,26},{12,28},{14,30},{16,0},... | collective-permute-start | bytes 442376 | tf_op jit(solution)/shard_map/ppermute | solution.py:553
  334.2 6.0 %collective-permute-start.40 = (bf16[96,768]{1,0:T(8,128)(2,1)S(1)}, bf16[96,768]{1,0:T(8,128)(2,1)S(1)}, u32[]{:S(2)}, u32[]{:S(2)}) collective-permute-start(bf16[96,768]{1,0:T(8,128)(2,1)S(1)} %fusion.19), channel_id=1, source_target_pairs={{0,1},{1,0},{2,3},{3,2},{4,5},{5,4},{6,7},{7,6},{8,9},{9,8},{10,11... | collective-permute-start | bytes 442376 | tf_op jit(solution)/shard_map/ppermute | solution.py:561
  335.7 7.7 %collective-permute-start.34 = (bf16[48,3072]{1,0:T(8,128)(2,1)S(1)}, bf16[48,3072]{1,0:T(8,128)(2,1)S(1)}, u32[]{:S(2)}, u32[]{:S(2)}) collective-permute-start(bf16[48,3072]{1,0:T(8,128)(2,1)S(1)} %fusion.16), channel_id=1, source_target_pairs={{0,1},{1,0},{2,3},{3,2},{4,5},{5,4},{6,7},{7,6},{8,9},{9,8},{10,11... | collective-permute-start | bytes 884744 | tf_op jit(solution)/shard_map/ppermute | solution.py:561
  (4 other events, 2.6 us)
